TPU v7x, 32 devices: a whole 2x2x4 slice. The times are simulated.
32 devices in a mesh: batch: 8 (over z, x), chan: 4 (over y, core).
Axes of the slice: x: 2, y: 2, z: 4, core: 2. Of those that a mesh axis runs over, the one named last changes fastest.
Arguments:
- inputs: bfloat16 [4, 64, 14, 14, 1024], P(None, 'batch', None, None, 'chan'), may hold values from -6 to 6
- weight_in: bfloat16 [1024, 512], P(None, 'chan'), may hold values from -0.1875 to 0.1875
- kernel_one: bfloat16 [3, 3, 512, 512], P(None, None, None, 'chan'), may hold values from -0.09375 to 0.09375
- weight_out: bfloat16 [512, 2048], P(None, 'chan'), may hold values from -0.25 to 0.25
- weight_skip: bfloat16 [1024, 2048], P(None, 'chan'), may hold values from -0.1875 to 0.1875
- second_in: bfloat16 [2048, 512], P(None, 'chan'), may hold values from -0.125 to 0.125
- kernel_two: bfloat16 [3, 3, 512, 512], P(None, None, None, 'chan'), may hold values from -0.09375 to 0.09375
- second_out: bfloat16 [512, 2048], P(None, 'chan'), may hold values from -0.25 to 0.25
- norm_reduce: float32 [2, 512], P(None, 'chan'), may hold values from 0.3 to 1.5
- norm_kernel: float32 [2, 512], P(None, 'chan'), may hold values from 0.3 to 1.5
- norm_expand: float32 [2, 2048], P(None, 'chan'), may hold values from 0.3 to 1.5
- norm_skip: float32 [2, 2048], P(None, 'chan'), may hold values from 0.3 to 1.5
- later_reduce: float32 [2, 512], P(None, 'chan'), may hold values from 0.3 to 1.5
- later_kernel: float32 [2, 512], P(None, 'chan'), may hold values from 0.3 to 1.5
- later_expand: float32 [2, 2048], P(None, 'chan'), may hold values from 0.3 to 1.5
- widths: int32 [4], replicated, may hold values from 256 to 512, as said below
- depths: int32 [4], replicated, may hold values from 1 to 2, as said below
- counts: int32 [4], replicated, may hold values from 32 to 64, as said below
- cotangent: bfloat16 [4, 64, 7, 7, 2048], P(None, 'batch', None, None, 'chan'), may hold values from -6 to 6
Outputs:
- result: bfloat16 [4, 64, 7, 7, 2048], P(None, 'batch', None, None, 'chan')
- inputs_grad: bfloat16 [4, 64, 14, 14, 1024], P(None, 'batch', None, None, 'chan')
- weight_in_grad: float32 [1024, 512], P('batch', 'chan')
- kernel_one_grad: float32 [3, 3, 512, 512], P(None, None, 'batch', 'chan')
- weight_out_grad: float32 [512, 2048], P('batch', 'chan')
- weight_skip_grad: float32 [1024, 2048], P('batch', 'chan')
- second_in_grad: float32 [2048, 512], P('batch', 'chan')
- kernel_two_grad: float32 [3, 3, 512, 512], P(None, None, 'batch', 'chan')
- second_out_grad: float32 [512, 2048], P('batch', 'chan')
- norm_reduce_grad: float32 [2, 512], P(None, 'chan')
- norm_kernel_grad: float32 [2, 512], P(None, 'chan')
- norm_expand_grad: float32 [2, 2048], P(None, 'chan')
- norm_skip_grad: float32 [2, 2048], P(None, 'chan')
- later_reduce_grad: float32 [2, 512], P(None, 'chan')
- later_kernel_grad: float32 [2, 512], P(None, 'chan')
- later_expand_grad: float32 [2, 2048], P(None, 'chan')
Inputs may be any that keep to these rules, and one draw needn't show every extreme that they name: widths[0] is 512 and widths[1] is 512/2 (the largest and smallest subnet). depths[0] is 2 and depths[1] is 1. live images of a subnet are its first counts[s] slots; counts[0] is 64 and counts[1] is 32.
All inputs are finite; a program needn't handle non-finite values.
Results may differ from a plain program's by a relative error of at most 0.025.
Values may be sent and summed in bfloat16 or wider, within the bound.
No kernel may reach another device: no remote copies, remote signals or barrier semaphores. Data moves between devices by JAX's collectives and lax.ppermute only.
A program may use at most 320 MiB of HBM per device.

v0:
```python
from functools import reduce

import jax
import jax.numpy as jnp
from jax import lax
from jax.sharding import PartitionSpec as P

epsilon = 1e-05


def as_sent(shard):

    def short(part):
        return part.astype(jnp.bfloat16) if part.dtype == jnp.float32 else part

    return jax.tree.map(short, shard)


def silu_grad(values):
    sigma = jax.nn.sigmoid(values)
    return sigma * (1.0 + values * (1.0 - sigma))


def gather_feat(active):
    return lax.all_gather(active, "chan", axis=4, tiled=True)


def spread_grad(partial_sum):
    return lax.psum_scatter(
        partial_sum.astype(jnp.bfloat16), "chan", scatter_dimension=4, tiled=True
    ).astype(jnp.float32)


def to_images(active):
    return lax.all_to_all(active, "chan", split_axis=1, concat_axis=4, tiled=True)


def to_channels(active):
    return lax.all_to_all(active, "chan", split_axis=4, concat_axis=1, tiled=True)


def channel_sums(first_sum, second_sum):
    return lax.psum((first_sum, second_sum), "batch")


def pointwise(active, weight):
    return jnp.einsum("sihwc,cd->sihwd", active, weight, preferred_element_type=jnp.float32)


def pointwise_back(gradient, weight):
    return jnp.einsum("sihwd,cd->sihwc", gradient, weight, preferred_element_type=jnp.float32)


def weight_back(active, gradient):
    return jnp.einsum("sihwc,sihwd->cd", active, gradient, preferred_element_type=jnp.float32)


def norm_forward(values, keep_mask, affine, pixels):
    masked = values * keep_mask
    first_sum, second_sum = channel_sums(
        jnp.sum(masked, axis=(1, 2, 3)), jnp.sum(masked * values, axis=(1, 2, 3))
    )
    average = first_sum / pixels
    variance = second_sum / pixels - average * average
    inv_std = lax.rsqrt(variance + epsilon)
    normed = (values - average[:, None, None, None, :]) * inv_std[:, None, None, None, :]
    return (keep_mask * (affine[0] * normed + affine[1]), normed, inv_std)


def norm_backward(gradient, keep_mask, affine, normed, inv_std, pixels):
    masked = gradient * keep_mask
    bias_sum, gain_sum = channel_sums(
        jnp.sum(masked, axis=(1, 2, 3)), jnp.sum(masked * normed, axis=(1, 2, 3))
    )
    factor = (affine[0] * inv_std)[:, None, None, None, :]
    spread = bias_sum[:, None, None, None, :] + normed * gain_sum[:, None, None, None, :]
    returned = factor * (masked - keep_mask * spread / pixels[:, None, None, None, :])
    return (returned, jnp.stack([jnp.sum(gain_sum, axis=0), jnp.sum(bias_sum, axis=0)]))


def patches(padded, stride, out_size):
    extent = stride * (out_size - 1) + 1
    pieces = []
    for row_off in range(3):
        for col_off in range(3):
            pieces.append(
                padded[
                    :, row_off : row_off + extent : stride, col_off : col_off + extent : stride, :
                ]
            )
    return jnp.concatenate(pieces, axis=3)


def fold_back(gradient, stride, out_size, height):
    channels = gradient.shape[3] // 9
    extent = stride * (out_size - 1) + 1
    summed = jnp.zeros((gradient.shape[0], height + 2, height + 2, channels), jnp.float32)
    for row_off in range(3):
        for col_off in range(3):
            offset = (row_off * 3 + col_off) * channels
            summed = summed.at[
                :, row_off : row_off + extent : stride, col_off : col_off + extent : stride, :
            ].add(gradient[:, :, :, offset : offset + channels])
    return summed[:, 1 : height + 1, 1 : height + 1, :]


def make_columns(active, stride, out_size):
    leading, per_lead = (active.shape[0], active.shape[1])
    flattened = active.reshape((leading * per_lead,) + active.shape[2:])
    padded = jnp.pad(flattened, ((0, 0), (1, 1), (1, 1), (0, 0)))
    return patches(padded, stride, out_size)


def spatial_forward(active, kernel, stride, out_size):
    leading, per_lead = (active.shape[0], active.shape[1])
    columns = make_columns(active, stride, out_size)
    width_all = columns.shape[3]
    output = jnp.dot(
        columns.reshape(-1, width_all),
        kernel.reshape(width_all, kernel.shape[3]),
        preferred_element_type=jnp.float32,
    )
    return (output.reshape(leading, per_lead, out_size, out_size, kernel.shape[3]), columns)


def spatial_backward(gradient, columns, kernel, stride, height):
    leading, per_lead, out_size = (gradient.shape[0], gradient.shape[1], gradient.shape[2])
    flat_grad = gradient.reshape(-1, gradient.shape[4])
    flat_cols = columns.reshape(-1, columns.shape[3])
    kernel_grad = jnp.einsum(
        "pk,po->ko", flat_cols, flat_grad, preferred_element_type=jnp.float32
    ).reshape(kernel.shape)
    col_grad = jnp.einsum(
        "po,ko->pk",
        flat_grad,
        kernel.reshape(-1, kernel.shape[3]),
        preferred_element_type=jnp.float32,
    )
    folded = fold_back(col_grad.reshape(columns.shape), stride, out_size, height)
    return (folded.reshape(leading, per_lead, height, height, folded.shape[3]), kernel_grad)


def subnet_pass(inputs, cotangent, widths, depths, counts, weights, kernels, norms):
    weight_in, weight_out, weight_skip, second_in, second_out = weights
    kernel_one, kernel_two = kernels
    norm_reduce, norm_kernel, norm_expand, norm_skip, later_reduce, later_kernel, later_expand = (
        norms
    )
    per_device = inputs.shape[1]
    narrow = weight_in.shape[1]
    in_size = inputs.shape[2]
    out_size = cotangent.shape[2]
    image_ids = lax.axis_index("batch") * per_device + jnp.arange(per_device, dtype=jnp.int32)
    channel_ids = lax.axis_index("chan") * narrow + jnp.arange(narrow, dtype=jnp.int32)
    live = (image_ids[None, :] < counts[:, None]).astype(jnp.float32)[:, :, None, None, None]
    width_live = (channel_ids[None, :] < widths[:, None]).astype(jnp.float32)[
        :, None, None, None, :
    ]
    inner_mask = live * width_live
    big_pixels = counts.astype(jnp.float32)[:, None] * (in_size * in_size)
    small_pixels = counts.astype(jnp.float32)[:, None] * (out_size * out_size)
    depth_on = (depths == 2).astype(jnp.float32)[:, None, None, None, None]
    full_in = gather_feat(inputs)
    pre_a, normed_a, inv_a = norm_forward(
        pointwise(full_in, weight_in), inner_mask, norm_reduce, big_pixels
    )
    act_a = jax.nn.silu(pre_a).astype(jnp.bfloat16)
    conv_b_img, columns_a = spatial_forward(to_images(act_a), kernel_one, 2, out_size)
    conv_b = to_channels(conv_b_img.astype(jnp.bfloat16)).astype(jnp.float32)
    pre_b, normed_b, inv_b = norm_forward(conv_b, inner_mask, norm_kernel, small_pixels)
    act_b = jax.nn.silu(pre_b).astype(jnp.bfloat16)
    full_b = gather_feat(act_b)
    skip_in = full_in[:, :, ::2, ::2, :]
    pre_c, normed_c, inv_c = norm_forward(
        pointwise(full_b, weight_out), live, norm_expand, small_pixels
    )
    pre_s, normed_s, inv_s = norm_forward(
        pointwise(skip_in, weight_skip), live, norm_skip, small_pixels
    )
    sum_one = pre_c + pre_s
    first_out = jax.nn.silu(sum_one)
    full_y = gather_feat(first_out.astype(jnp.bfloat16))
    pre_d, normed_d, inv_d = norm_forward(
        pointwise(full_y, second_in), inner_mask, later_reduce, small_pixels
    )
    act_d = jax.nn.silu(pre_d).astype(jnp.bfloat16)
    conv_e_img, columns_d = spatial_forward(to_images(act_d), kernel_two, 1, out_size)
    conv_e = to_channels(conv_e_img.astype(jnp.bfloat16)).astype(jnp.float32)
    pre_e, normed_e, inv_e = norm_forward(conv_e, inner_mask, later_kernel, small_pixels)
    act_e = jax.nn.silu(pre_e).astype(jnp.bfloat16)
    full_e = gather_feat(act_e)
    pre_f, normed_f, inv_f = norm_forward(
        pointwise(full_e, second_out), live, later_expand, small_pixels
    )
    sum_two = pre_f + first_out
    second_val = jax.nn.silu(sum_two)
    result = first_out + depth_on * (second_val - first_out)
    grad_out = cotangent.astype(jnp.float32)
    grad_sum_two = depth_on * grad_out * silu_grad(sum_two)
    grad_first = (1.0 - depth_on) * grad_out + grad_sum_two
    grad_cf, stats_f = norm_backward(
        grad_sum_two, live, later_expand, normed_f, inv_f, small_pixels
    )
    grad_cf_low = grad_cf.astype(jnp.bfloat16)
    grad_wf = weight_back(full_e, grad_cf_low)
    grad_act_e = spread_grad(pointwise_back(grad_cf_low, second_out))
    grad_ce, stats_e = norm_backward(
        grad_act_e * silu_grad(pre_e), inner_mask, later_kernel, normed_e, inv_e, small_pixels
    )
    grad_ce_low = grad_ce.astype(jnp.bfloat16)
    grad_ce_img = to_images(grad_ce_low)
    grad_act_d_img, grad_kernel_two = spatial_backward(
        grad_ce_img, columns_d, kernel_two, 1, out_size
    )
    grad_act_d = to_channels(grad_act_d_img.astype(jnp.bfloat16)).astype(jnp.float32)
    grad_cd, stats_d = norm_backward(
        grad_act_d * silu_grad(pre_d), inner_mask, later_reduce, normed_d, inv_d, small_pixels
    )
    grad_cd_low = grad_cd.astype(jnp.bfloat16)
    grad_wd = weight_back(full_y, grad_cd_low)
    grad_first = grad_first + spread_grad(pointwise_back(grad_cd_low, second_in))
    grad_sum_one = grad_first * silu_grad(sum_one)
    grad_cc, stats_c = norm_backward(grad_sum_one, live, norm_expand, normed_c, inv_c, small_pixels)
    grad_cs, stats_s = norm_backward(grad_sum_one, live, norm_skip, normed_s, inv_s, small_pixels)
    grad_cc_low = grad_cc.astype(jnp.bfloat16)
    grad_cs_low = grad_cs.astype(jnp.bfloat16)
    grad_wc = weight_back(full_b, grad_cc_low)
    grad_ws = weight_back(skip_in, grad_cs_low)
    grad_act_b = spread_grad(pointwise_back(grad_cc_low, weight_out))
    grad_cb, stats_b = norm_backward(
        grad_act_b * silu_grad(pre_b), inner_mask, norm_kernel, normed_b, inv_b, small_pixels
    )
    grad_cb_low = grad_cb.astype(jnp.bfloat16)
    grad_cb_img = to_images(grad_cb_low)
    grad_act_a_img, grad_kernel_one = spatial_backward(
        grad_cb_img, columns_a, kernel_one, 2, in_size
    )
    grad_act_a = to_channels(grad_act_a_img.astype(jnp.bfloat16)).astype(jnp.float32)
    grad_ca, stats_a = norm_backward(
        grad_act_a * silu_grad(pre_a), inner_mask, norm_reduce, normed_a, inv_a, big_pixels
    )
    grad_ca_low = grad_ca.astype(jnp.bfloat16)
    grad_wa = weight_back(full_in, grad_ca_low)
    part_in = pointwise_back(grad_ca_low, weight_in)
    part_in = part_in.at[:, :, ::2, ::2, :].add(pointwise_back(grad_cs_low, weight_skip))
    grad_in = spread_grad(part_in)
    return (
        result,
        grad_in,
        (grad_wa, grad_wc, grad_ws, grad_wd, grad_wf),
        (grad_kernel_one, grad_kernel_two),
        (stats_a, stats_b, stats_c, stats_s, stats_d, stats_e, stats_f),
    )


def add_all(*pieces):
    return reduce(jnp.add, pieces)


def body(
    inputs,
    weight_in,
    kernel_one,
    weight_out,
    weight_skip,
    second_in,
    kernel_two,
    second_out,
    norm_reduce,
    norm_kernel,
    norm_expand,
    norm_skip,
    later_reduce,
    later_kernel,
    later_expand,
    widths,
    depths,
    counts,
    cotangent,
):
    kernels = (
        lax.all_gather(kernel_one, "chan", axis=3, tiled=True),
        lax.all_gather(kernel_two, "chan", axis=3, tiled=True),
    )
    weights = (weight_in, weight_out, weight_skip, second_in, second_out)
    norms = (
        norm_reduce,
        norm_kernel,
        norm_expand,
        norm_skip,
        later_reduce,
        later_kernel,
        later_expand,
    )
    outcomes = []
    for member in range(inputs.shape[0]):
        outcomes.append(
            subnet_pass(
                inputs[member : member + 1],
                cotangent[member : member + 1],
                widths[member : member + 1],
                depths[member : member + 1],
                counts[member : member + 1],
                weights,
                kernels,
                norms,
            )
        )
    result = jnp.concatenate([outcome[0] for outcome in outcomes], axis=0)
    grad_in = jnp.concatenate([outcome[1] for outcome in outcomes], axis=0)
    weight_grads = jax.tree.map(add_all, *[outcome[2] for outcome in outcomes])
    kernel_grads = jax.tree.map(add_all, *[outcome[3] for outcome in outcomes])
    norm_grads = jax.tree.map(add_all, *[outcome[4] for outcome in outcomes])
    weight_sums = jax.tree.map(
        lambda part: part.astype(jnp.float32),
        lax.psum_scatter(as_sent(weight_grads), "batch", scatter_dimension=0, tiled=True),
    )
    chan_sums = jax.tree.map(
        lambda part: part.astype(jnp.float32),
        lax.psum_scatter(as_sent(kernel_grads), "chan", scatter_dimension=3, tiled=True),
    )
    kernel_sums = jax.tree.map(
        lambda part: part.astype(jnp.float32),
        lax.psum_scatter(as_sent(chan_sums), "batch", scatter_dimension=2, tiled=True),
    )
    return (
        result.astype(jnp.bfloat16),
        grad_in.astype(jnp.bfloat16),
        weight_sums[0],
        kernel_sums[0],
        weight_sums[1],
        weight_sums[2],
        weight_sums[3],
        kernel_sums[1],
        weight_sums[4],
        norm_grads[0],
        norm_grads[1],
        norm_grads[2],
        norm_grads[3],
        norm_grads[4],
        norm_grads[5],
        norm_grads[6],
    )


def solution(mesh):
    in_specs = (
        P(None, "batch", None, None, "chan"),
        P(None, "chan"),
        P(None, None, None, "chan"),
        P(None, "chan"),
        P(None, "chan"),
        P(None, "chan"),
        P(None, None, None, "chan"),
        P(None, "chan"),
        P(None, "chan"),
        P(None, "chan"),
        P(None, "chan"),
        P(None, "chan"),
        P(None, "chan"),
        P(None, "chan"),
        P(None, "chan"),
        P(),
        P(),
        P(),
        P(None, "batch", None, None, "chan"),
    )
    out_specs = (
        P(None, "batch", None, None, "chan"),
        P(None, "batch", None, None, "chan"),
        P("batch", "chan"),
        P(None, None, "batch", "chan"),
        P("batch", "chan"),
        P("batch", "chan"),
        P("batch", "chan"),
        P(None, None, "batch", "chan"),
        P("batch", "chan"),
        P(None, "chan"),
        P(None, "chan"),
        P(None, "chan"),
        P(None, "chan"),
        P(None, "chan"),
        P(None, "chan"),
        P(None, "chan"),
    )
    return jax.shard_map(body, mesh=mesh, in_specs=in_specs, out_specs=out_specs, check_vma=False)
```

profile of v0, /device:TPU:0, one launch (start us, length us, event | category | flops | bytes accessed | tf_op | source)
XLA Modules:
  0.0 2749.2 jit_solution(1652547178463312345)
XLA Ops:
  26.1 19.2 all-gather.15.cloned.1.call-done
  49.5 30.0 %all-gather.21.cloned.1.call-done = bf16[1,8,14,14,1024]{4,3,2,1,0:T(8,128)(2,1)} async-done(((bf16[1,8,14,14,256]{4,3,2,1,0:T(8,128)(2,1)}), bf16[1,8,14,14,1024]{4,3,2,1,0:T(8,128)(2,1)}) %all-gather.21.cloned.1.call-update) | async-done | bytes 3211280 | tf_op jit(solution)/shard_map/all_gather | solution.py:25
  82.7 30.4 %all-gather.23.cloned.1.call-done = bf16[1,8,14,14,1024]{4,3,2,1,0:T(8,128)(2,1)} async-done(((bf16[1,8,14,14,256]{4,3,2,1,0:T(8,128)(2,1)}), bf16[1,8,14,14,1024]{4,3,2,1,0:T(8,128)(2,1)}) %all-gather.23.cloned.1.call-update) | async-done | bytes 3211280 | tf_op jit(solution)/shard_map/all_gather | solution.py:25
  116.3 30.2 %all-gather.25.cloned.1.call-done = bf16[1,8,14,14,1024]{4,3,2,1,0:T(8,128)(2,1)} async-done(((bf16[1,8,14,14,256]{4,3,2,1,0:T(8,128)(2,1)}), bf16[1,8,14,14,1024]{4,3,2,1,0:T(8,128)(2,1)}) %all-gather.25.cloned.1.call-update) | async-done | bytes 3211280 | tf_op jit(solution)/shard_map/all_gather | solution.py:25
  150.6 21.3 all-reduce.23
  193.5 28.1 %slice.1832 = bf16[1,8,7,7,1024]{4,3,2,1,0:T(8,128)(2,1)} slice(bf16[1,8,14,14,1024]{4,3,2,1,0:T(8,128)(2,1)} %all-gather.15.cloned.1.call-done), slice={[0:1:1], [0:8:1], [0:14:2], [0:14:2], [0:1024:1]} | slice | bytes 1605632 | tf_op jit(solution)/shard_map/slice | solution.py:173
  227.9 28.1 %slice.1861 = bf16[1,8,7,7,1024]{4,3,2,1,0:T(8,128)(2,1)} slice(bf16[1,8,14,14,1024]{4,3,2,1,0:T(8,128)(2,1)} %all-gather.21.cloned.1.call-done), slice={[0:1:1], [0:8:1], [0:14:2], [0:14:2], [0:1024:1]} | slice | bytes 1605632 | tf_op jit(solution)/shard_map/slice | solution.py:173
  256.0 28.1 %slice.1883 = bf16[1,8,7,7,1024]{4,3,2,1,0:T(8,128)(2,1)} slice(bf16[1,8,14,14,1024]{4,3,2,1,0:T(8,128)(2,1)} %all-gather.23.cloned.1.call-done), slice={[0:1:1], [0:8:1], [0:14:2], [0:14:2], [0:1024:1]} | slice | bytes 1605632 | tf_op jit(solution)/shard_map/slice | solution.py:173
  304.5 28.1 %slice.1905 = bf16[1,8,7,7,1024]{4,3,2,1,0:T(8,128)(2,1)} slice(bf16[1,8,14,14,1024]{4,3,2,1,0:T(8,128)(2,1)} %all-gather.25.cloned.1.call-done), slice={[0:1:1], [0:8:1], [0:14:2], [0:14:2], [0:1024:1]} | slice | bytes 1605632 | tf_op jit(solution)/shard_map/slice | solution.py:173
  568.9 21.6 all-reduce.22
  624.8 33.1 %all-reduce.21 = (f32[1,512]{1,0:T(1,128)S(1)}, f32[1,512]{1,0:T(1,128)S(1)}, f32[1,512]{1,0:T(1,128)S(1)}, f32[1,512]{1,0:T(1,128)S(1)}, f32[1,512]{1,0:T(1,128...) all-reduce(f32[1,512]{1,0:T(1,128)S(1)} %bitcast.1997, ...), channel_id=1, replica_groups=mesh['batch'=8,'chan'=4] {'batch'}, use_global_device_ids=true, to_apply=%region_13.14 | all-reduce | flops 8192 | bytes 65536 | tf_op jit(solution)/shard_map/psum | solution.py:43
  681.7 19.4 all-gather.29.cloned.1.call-done
  703.1 20.0 all-gather.31.cloned.1.call-done
  725.1 20.0 all-gather.33.cloned.1.call-done
  747.1 21.4 all-reduce.20
  921.3 18.3 all-reduce.19
  977.2 34.2 %all-reduce.18 = (f32[1,512]{1,0:T(1,128)S(1)}, f32[1,512]{1,0:T(1,128)S(1)}, f32[1,512]{1,0:T(1,128)S(1)}, f32[1,512]{1,0:T(1,128)S(1)}, f32[1,512]{1,0:T(1,128...) all-reduce(f32[1,512]{1,0:T(1,128)} %bitcast.2012, ...), channel_id=1, replica_groups=mesh['batch'=8,'chan'=4] {'batch'}, use_global_device_ids=true, to_apply=%region_25.26 | all-reduce | flops 4096 | bytes 32768 | tf_op jit(solution)/shard_map/psum | solution.py:43
  1019.4 33.6 %all-reduce.17 = (f32[1,512]{1,0:T(1,128)S(1)}, f32[1,512]{1,0:T(1,128)S(1)}, f32[1,512]{1,0:T(1,128)S(1)}, f32[1,512]{1,0:T(1,128)S(1)}, f32[1,512]{1,0:T(1,128...) all-reduce(f32[1,512]{1,0:T(1,128)S(1)} %bitcast.1797, ...), channel_id=1, replica_groups=mesh['batch'=8,'chan'=4] {'batch'}, use_global_device_ids=true, to_apply=%region_115.116 | all-reduce | flops 4096 | bytes 32768 | tf_op jit(solution)/shard_map/psum | solution.py:43
  1144.4 18.9 reduce-scatter.88.cloned.1.call-done
  1171.6 21.8 all-reduce.16
  1425.4 17.1 all-reduce.15
  1519.0 15.7 reduce-scatter.58.cloned.1.call-done
  1538.8 26.8 reduce-scatter.62.cloned.1.call-done
  1569.9 37.6 %all-reduce.14 = (f32[1,512]{1,0:T(1,128)S(1)}, f32[1,512]{1,0:T(1,128)S(1)}, f32[1,512]{1,0:T(1,128)S(1)}, f32[1,512]{1,0:T(1,128)S(1)}, f32[1,512]{1,0:T(1,128...) all-reduce(f32[1,512]{1,0:T(1,128)S(1)} %bitcast.1789, ...), channel_id=1, replica_groups=mesh['batch'=8,'chan'=4] {'batch'}, use_global_device_ids=true, to_apply=%region_130.131 | all-reduce | flops 4096 | bytes 32768 | tf_op jit(solution)/shard_map/psum | solution.py:43
  1759.0 17.1 all-reduce.13
  2256.1 35.7 %all-reduce.12 = (f32[1,128]{1,0:T(1,128)S(1)}, f32[1,128]{1,0:T(1,128)S(1)}, f32[1,128]{1,0:T(1,128)S(1)}, f32[1,128]{1,0:T(1,128)S(1)}, f32[1,128]{1,0:T(1,128...) all-reduce(f32[1,128]{1,0:T(1,128)S(1)} %bitcast.1954, ...), channel_id=1, replica_groups=mesh['batch'=8,'chan'=4] {'batch'}, use_global_device_ids=true, to_apply=%region_148.149 | all-reduce | flops 3072 | bytes 24576 | tf_op jit(solution)/shard_map/psum | solution.py:43
  2444.1 38.6 %reduce-scatter.64.cloned.1.call-done = bf16[1,8,14,14,256]{4,1,3,2,0:T(8,128)(2,1)} async-done(((bf16[1,8,14,14,1024]{4,1,3,2,0:T(8,128)(2,1)}), bf16[1,8,14,14,256]{4,1,3,2,0:T(8,128)(2,1)}) %reduce-scatter.64.cloned.1.call-update) | async-done | bytes 802832 | tf_op jit(solution)/shard_map/reduce_scatter | solution.py:29
  2482.6 41.1 %reduce-scatter.60.cloned.1.call-done = bf16[1,8,14,14,256]{4,1,3,2,0:T(8,128)(2,1)} async-done(((bf16[1,8,14,14,1024]{4,1,3,2,0:T(8,128)(2,1)}), bf16[1,8,14,14,256]{4,1,3,2,0:T(8,128)(2,1)}) %reduce-scatter.60.cloned.1.call-update) | async-done | bytes 802832 | tf_op jit(solution)/shard_map/reduce_scatter | solution.py:29
  2523.7 41.0 %reduce-scatter.56.cloned.1.call-done = bf16[1,8,14,14,256]{4,1,3,2,0:T(8,128)(2,1)} async-done(((bf16[1,8,14,14,1024]{4,1,3,2,0:T(8,128)(2,1)}), bf16[1,8,14,14,256]{4,1,3,2,0:T(8,128)(2,1)}) %reduce-scatter.56.cloned.1.call-update) | async-done | bytes 802832 | tf_op jit(solution)/shard_map/reduce_scatter | solution.py:29
  2564.7 40.9 %reduce-scatter.52.cloned.1.call-done = bf16[1,8,14,14,256]{4,1,3,2,0:T(8,128)(2,1)} async-done(((bf16[1,8,14,14,1024]{4,1,3,2,0:T(8,128)(2,1)}), bf16[1,8,14,14,256]{4,1,3,2,0:T(8,128)(2,1)}) %reduce-scatter.52.cloned.1.call-update) | async-done | bytes 802832 | tf_op jit(solution)/shard_map/reduce_scatter | solution.py:29
  2608.9 64.8 %reduce-scatter.72.cloned.1.call-done = bf16[3,3,64,128]{3,2,1,0:T(8,128)(2,1)} async-done(((bf16[3,3,512,128]{3,2,1,0:T(8,128)(2,1)}), bf16[3,3,64,128]{3,2,1,0:T(8,128)(2,1)}) %reduce-scatter.72.cloned.1.call-update) | async-done | bytes 147472 | tf_op jit(solution)/shard_map/reduce_scatter | solution.py:324
  2675.4 65.4 %reduce-scatter.66.cloned.1.call-done = bf16[3,3,64,128]{3,2,1,0:T(8,128)(2,1)} async-done(((bf16[3,3,512,128]{3,2,1,0:T(8,128)(2,1)}), bf16[3,3,64,128]{3,2,1,0:T(8,128)(2,1)}) %reduce-scatter.66.cloned.1.call-update) | async-done | bytes 147472 | tf_op jit(solution)/shard_map/reduce_scatter | solution.py:324
  (2020 shorter events, 1772.2 us)
Async XLA Ops:
  10.5 69.0 %all-gather.21.cloned.1.call-start = ((), (), s32[]{:S(2)}) async-start(), calls=%async_computation.60 | async-start | bytes 4587520 | tf_op jit(solution)/shard_map/all_gather | solution.py:25
  11.7 101.4 %all-gather.23.cloned.1.call-start = ((), (), s32[]{:S(2)}) async-start(), calls=%async_computation.61 | async-start | bytes 4587520 | tf_op jit(solution)/shard_map/all_gather | solution.py:25
  12.9 133.6 %all-gather.25.cloned.1.call-start = ((), (), s32[]{:S(2)}) async-start(), calls=%async_computation.62 | async-start | bytes 4587520 | tf_op jit(solution)/shard_map/all_gather | solution.py:25
  14.1 466.8 %all-gather.17.cloned.1.call-start = ((), (), s32[]{:S(2)}) async-start(), calls=%async_computation.58 | async-start | bytes 5898240 | tf_op jit(solution)/shard_map/all_gather | solution.py:282
  286.9 140.1 %all-to-all-start.8 = ((bf16[1,8,14,14,128]{4,3,2,0,1:T(8,128)(2,1)}), bf16[1,8,14,14,128]{4,3,2,0,1:T(8,128)(2,1)S(1)}, u32[]{:S(2)}, u32[]{:S(2)}) async-start(bf16[1,8,14,14,128]{4,3,2,0,1:T(8,128)(2,1)} %get-tuple-element.1062), calls=%async_computation.8 | async-start | bytes 917504 | tf_op jit(solution)/shard_map/all_to_all | solution.py:35
  549.4 130.2 %all-gather.27.cloned.1.call-start = ((), (), s32[]{:S(2)}) async-start(), calls=%async_computation.76 | async-start | bytes 2007040 | tf_op jit(solution)/shard_map/all_gather | solution.py:25
  667.4 77.8 %all-gather.33.cloned.1.call-start = ((), (), s32[]{:S(2)}) async-start(), calls=%async_computation.79 | async-start | bytes 2007040 | tf_op jit(solution)/shard_map/all_gather | solution.py:25
  668.1 130.9 %all-gather.19.cloned.1.call-start = ((), (), s32[]{:S(2)}) async-start(), calls=%async_computation.59 | async-start | bytes 5898240 | tf_op jit(solution)/shard_map/all_gather | solution.py:283
  896.3 232.5 %reduce-scatter.76.cloned.1.call-start = ((), (), s32[]{:S(2)}) async-start(), calls=%async_computation.80 | async-start | bytes 655360
  1386.9 123.3 %reduce-scatter.50.cloned.1.call-start = ((), (), s32[]{:S(2)}) async-start(), calls=%async_computation.63 | async-start | bytes 2007040 | tf_op jit(solution)/shard_map/reduce_scatter | solution.py:29
  1444.6 70.1 %reduce-scatter.54.cloned.1.call-start = ((), (), s32[]{:S(2)}) async-start(), calls=%async_computation.65 | async-start | bytes 2007040 | tf_op jit(solution)/shard_map/reduce_scatter | solution.py:29
  1446.6 88.1 %reduce-scatter.58.cloned.1.call-start = ((), (), s32[]{:S(2)}) async-start(), calls=%async_computation.67 | async-start | bytes 2007040 | tf_op jit(solution)/shard_map/reduce_scatter | solution.py:29
  1449.3 116.4 %reduce-scatter.62.cloned.1.call-start = ((), (), s32[]{:S(2)}) async-start(), calls=%async_computation.69 | async-start | bytes 2007040 | tf_op jit(solution)/shard_map/reduce_scatter | solution.py:29
  1491.9 242.9 %reduce-scatter.78.cloned.1.call-start = ((), (), s32[]{:S(2)}) async-start(), calls=%async_computation.81 | async-start | bytes 655360
  1626.4 113.6 %reduce-scatter.82.cloned.1.call-start = ((), (), s32[]{:S(2)}) async-start(), calls=%async_computation.83 | async-start | bytes 655360
  1650.2 94.9 %reduce-scatter.86.cloned.1.call-start = ((), (), s32[]{:S(2)}) async-start(), calls=%async_computation.85 | async-start | bytes 655360
  1673.7 76.8 %reduce-scatter.90.cloned.1.call-start = ((), (), s32[]{:S(2)}) async-start(), calls=%async_computation.87 | async-start | bytes 655360
  1697.1 706.4 %reduce-scatter.98.cloned.1.call-start = ((), (), s32[]{:S(2)}) async-start(), calls=%async_computation.91 | async-start | bytes 5898240
  1804.7 603.8 %reduce-scatter.94.cloned.1.call-start = ((), (), s32[]{:S(2)}) async-start(), calls=%async_computation.89 | async-start | bytes 5898240
  1868.0 555.5 %reduce-scatter.74.cloned.1.call-start = ((), (), s32[]{:S(2)}) async-start(), calls=%async_computation.75 | async-start | bytes 589824 | tf_op jit(solution)/shard_map/reduce_scatter | solution.py:316
  1876.0 549.0 %reduce-scatter.70.cloned.1.call-start = ((), (), s32[]{:S(2)}) async-start(), calls=%async_computation.73 | async-start | bytes 589824 | tf_op jit(solution)/shard_map/reduce_scatter | solution.py:316
  1949.2 136.4 %all-to-all-start.27 = ((bf16[4,2,25088]{2,1,0:T(2,128)(2,1)}), bf16[4,2,25088]{2,1,0:T(2,128)(2,1)S(1)}, u32[]{:S(2)}, u32[]{:S(2)}) async-start(bf16[4,2,25088]{2,1,0:T(2,128)(2,1)} %reshape.4784), calls=%async_computation.32 | async-start | bytes 802816 | tf_op jit(solution)/shard_map/all_to_all | solution.py:39
  2097.5 66.3 %all-to-all-start.31 = ((bf16[4,2,25088]{2,1,0:T(2,128)(2,1)}), bf16[4,2,25088]{2,1,0:T(2,128)(2,1)}, u32[]{:S(2)}, u32[]{:S(2)}) async-start(bf16[4,2,25088]{2,1,0:T(2,128)(2,1)} %reshape.4792), calls=%async_computation.38 | async-start | bytes 802816 | tf_op jit(solution)/shard_map/all_to_all | solution.py:39
  2167.2 260.0 %reduce-scatter.68.cloned.1.call-start = ((), (), s32[]{:S(2)}) async-start(), calls=%async_computation.72 | async-start | bytes 589824 | tf_op jit(solution)/shard_map/reduce_scatter | solution.py:316
  2169.8 260.1 %reduce-scatter.92.cloned.1.call-start = ((), (), s32[]{:S(2)}) async-start(), calls=%async_computation.88 | async-start | bytes 294912
  2316.7 125.5 %reduce-scatter.96.cloned.1.call-start = ((), (), s32[]{:S(2)}) async-start(), calls=%async_computation.90 | async-start | bytes 1179648
  2322.2 160.4 %reduce-scatter.64.cloned.1.call-start = ((), (), s32[]{:S(2)}) async-start(), calls=%async_computation.70 | async-start | bytes 4014080 | tf_op jit(solution)/shard_map/reduce_scatter | solution.py:29
  2343.6 180.2 %reduce-scatter.60.cloned.1.call-start = ((), (), s32[]{:S(2)}) async-start(), calls=%async_computation.68 | async-start | bytes 4014080 | tf_op jit(solution)/shard_map/reduce_scatter | solution.py:29
  2363.6 201.1 %reduce-scatter.56.cloned.1.call-start = ((), (), s32[]{:S(2)}) async-start(), calls=%async_computation.66 | async-start | bytes 4014080 | tf_op jit(solution)/shard_map/reduce_scatter | solution.py:29
  2383.5 222.2 %reduce-scatter.52.cloned.1.call-start = ((), (), s32[]{:S(2)}) async-start(), calls=%async_computation.64 | async-start | bytes 4014080 | tf_op jit(solution)/shard_map/reduce_scatter | solution.py:29
  2403.5 270.2 %reduce-scatter.72.cloned.1.call-start = ((), (), s32[]{:S(2)}) async-start(), calls=%async_computation.74 | async-start | bytes 1327104 | tf_op jit(solution)/shard_map/reduce_scatter | solution.py:324
  2408.4 332.4 %reduce-scatter.66.cloned.1.call-start = ((), (), s32[]{:S(2)}) async-start(), calls=%async_computation.71 | async-start | bytes 1327104 | tf_op jit(solution)/shard_map/reduce_scatter | solution.py:324
  (574 other events, 17229.1 us)
Sparse Core Ops, SparseCore 0:
  10.7 34.6 all-gather.14
  47.5 31.9 all-gather.20
  81.1 31.9 all-gather.22
  114.5 31.9 all-gather.24
  147.9 38.6 all-gather.16
  681.2 19.8 all-gather.28
  703.2 19.8 all-gather.30
  725.2 19.8 all-gather.32
  746.5 39.2 all-gather.18
  1093.2 21.6 reduce-scatter.79
  1117.4 21.6 reduce-scatter.83
  1141.6 21.6 reduce-scatter.87
  1444.7 27.5 reduce-scatter.49
  1475.4 28.3 reduce-scatter.53
  1506.2 28.4 reduce-scatter.57
  1537.3 28.3 reduce-scatter.61
  1650.3 18.8 reduce-scatter.81
  1673.8 19.6 reduce-scatter.85
  1697.2 20.4 reduce-scatter.89
  1734.8 44.0 reduce-scatter.97
  1868.2 46.9 reduce-scatter.93
  1918.5 61.9 reduce-scatter.73
  1984.0 60.9 reduce-scatter.69
  2171.1 61.4 reduce-scatter.67
  2316.8 58.9 reduce-scatter.91
  2379.6 62.5 reduce-scatter.95
  2445.2 37.3 reduce-scatter.63
  2485.3 38.3 reduce-scatter.59
  2526.3 38.3 reduce-scatter.55
  2567.3 38.3 reduce-scatter.51
  2609.1 64.6 reduce-scatter.71
  2677.2 63.6 reduce-scatter.65
  (3 shorter events, 53.2 us)
where the time goes:
time: 2780 us; the launch traced here: 2750 us
  local copies, waits for them, and re-layouts  1030 us (37%)
  waiting for transfers between devices  574 us (21%)
  other arithmetic  392 us (14%)
  blocking collectives  367 us (13%)
  matrix products  224 us (8%)
  starting transfers between devices  132 us (5%)
  between operations  29 us (1%)
    unnamed x1264, local copies, waits for them, and re-layouts  512 us
    psum x12, blocking collectives, channel_sums(): return lax.psum((first_sum, second_sum), 'batch')  313 us
    reduce_scatter x8, waiting for transfers between devices, spread_grad(): lax.psum_scatter(partial_sum.astype(jnp.bfloat16), 'chan', scatter_dimens...  204 us
    all_gather x8, waiting for transfers between devices, gather_feat(): return lax.all_gather(active, 'chan', axis=4, tiled=True)  180 us
    scatter-add x36, other arithmetic, fold_back(): summed = summed.at[:, row_off:row_off + extent:stride, col_off:col_off +...  166 us
    reduce_scatter x2, waiting for transfers between devices, body(): lax.psum_scatter(as_sent(chan_sums), 'batch', scatter_dimension=2, tiled=...  130 us
    slice x40, local copies, waits for them, and re-layouts, patches(): padded[:, row_off:row_off + extent:stride, col_off:col_off + extent:strid...  113 us
    slice x4, local copies, waits for them, and re-layouts, subnet_pass(): skip_in = full_in[:, :, ::2, ::2, :]  113 us
  transfers between devices with their start and end apart: 67, of which 25 were waited for; matrix products, arithmetic and copies ran while one was open for 54% of the time, Pallas kernels for 0%

commit v1 on v0

v1 whole, which is shorter than its diff:
```python
import jax
import jax.numpy as jnp
from jax import lax
from jax.experimental import pallas as pl
from jax.experimental.pallas import tpu as pltpu
from jax.sharding import PartitionSpec as P

EPS = 1e-05
F32 = jnp.float32
BF = jnp.bfloat16
MID = 512
Q = 4
R = 392
NT = (((1,), (1,)), ((), ()))
TN = (((0,), (0,)), ((), ()))
VMEM_LIMIT = 48 * 1024 * 1024


def call(body, grid, ins, outs, scratch=(), flops=0, moved=0):
    in_specs = []
    for item in ins:
        if item[1] is None:
            in_specs.append(pl.BlockSpec(memory_space=pltpu.SMEM))
        else:
            in_specs.append(pl.BlockSpec(item[1], item[2]))
    return pl.pallas_call(
        body,
        grid=grid,
        in_specs=in_specs,
        out_specs=[pl.BlockSpec(item[2], item[3]) for item in outs],
        out_shape=[jax.ShapeDtypeStruct(item[0], item[1]) for item in outs],
        scratch_shapes=list(scratch),
        compiler_params=pltpu.CompilerParams(vmem_limit_bytes=VMEM_LIMIT),
        cost_estimate=pl.CostEstimate(flops=int(flops), bytes_accessed=int(moved), transcendentals=0),
    )(*[item[0] for item in ins])


def whole(array):
    zeros = (0,) * array.ndim
    return (array, array.shape, lambda i: zeros)


def bands():
    return [slice(56 * h, 56 * h + 56) for h in range(7)]


def tall(value):
    return value.reshape(7, 8, value.shape[-1])


def dot(left, right, dims=(((1,), (0,)), ((), ()))):
    return lax.dot_general(left, right, dims, preferred_element_type=F32)


def mean_inv(sums, pixels):
    total = jnp.sum(sums, axis=0)
    mean = total[:, :MID] / pixels
    var = jnp.maximum(total[:, MID : 2 * MID] / pixels - mean * mean, 0.0)
    return mean, lax.rsqrt(var + EPS)


def forward_coef(sums, affine, mask, pixels):
    mean, inv = mean_inv(sums, pixels)
    scale = affine[0:1] * inv
    return mask * scale, mask * (affine[1:2] - mean * scale), mean, inv


def backward_coef(sums, grad_sums, which, affine, mask, pixels):
    mean, inv = mean_inv(sums, pixels)
    total = jnp.sum(grad_sums, axis=0)
    first = total[:, :MID] / pixels
    second = total[:, which * MID : (which + 1) * MID] / pixels
    scale = affine[0:1] * inv
    slope = -scale * second * inv
    return mask * scale, mask * slope, mask * (-scale * first - slope * mean)


def silu(u):
    return u * jax.nn.sigmoid(u)


def silu_both(u):
    s = jax.nn.sigmoid(u)
    return u * s, s * (1.0 + u * (1.0 - s))


def silu_slope(u):
    s = jax.nn.sigmoid(u)
    return s * (1.0 + u * (1.0 - s))


def fold(acc, value):
    return acc + jnp.sum(tall(value), axis=0)


def put_sums(ref, parts):
    row = jnp.concatenate([jnp.sum(part, axis=0, keepdims=True) for part in parts], axis=1)
    ref[...] = jnp.broadcast_to(row[None], ref.shape)


def value_sums(out_ref, pieces, live):
    first = jnp.zeros((8, MID), F32)
    second = jnp.zeros((8, MID), F32)
    for value in pieces:
        first = fold(first, value)
        second = fold(second, value * value)
    put_sums(out_ref, [first * live, second * live])


def rows_in(inputs):
    subnets, images, size, _, width = inputs.shape
    cut = inputs.reshape(subnets, images, size // 2, 2, size // 2, 2, width)
    return jnp.transpose(cut, (0, 3, 5, 2, 4, 1, 6)).reshape(subnets, 4, R, width)


def rows_out(rows, subnets):
    cut = rows.reshape(subnets, 2, 2, 7, 7, 8, rows.shape[3])
    return jnp.transpose(cut, (0, 5, 3, 1, 4, 2, 6)).reshape(subnets, 8, 14, 14, rows.shape[3])


def small_in(maps):
    return jnp.transpose(maps, (0, 2, 3, 1, 4)).reshape(maps.shape[0], R, maps.shape[4])


def small_out(rows, subnets):
    return jnp.transpose(rows.reshape(subnets, 7, 7, 8, rows.shape[2]), (0, 3, 1, 2, 4))


def lanes(ref):
    return jnp.concatenate([ref[j] for j in range(ref.shape[0])], axis=1)


def stage_a(slabs, weight, live, nb):
    nch, width = slabs.shape[0], slabs.shape[3]
    cin = nch * width

    def body(x_ref, w_ref, live_ref, a_ref, s_ref, sums):
        p = pl.program_id(0)
        x = jnp.concatenate([x_ref[k, 0] for k in range(nch)], axis=1)
        w = lanes(w_ref)
        value = dot(x, w)
        a_ref[0] = value

        @pl.when(p == 0)
        def _():
            sums[...] = jnp.zeros_like(sums)

        first = jnp.zeros((8, MID), F32)
        second = jnp.zeros((8, MID), F32)
        for band in bands():
            piece = value[band]
            first = fold(first, piece)
            second = fold(second, piece * piece)
        sums[0] += first
        sums[1] += second

        @pl.when(p == 3)
        def _():
            put_sums(s_ref, [sums[0] * live_ref[...], sums[1] * live_ref[...]])

    return call(
        body,
        (4,),
        [(slabs, (nch, 1, R, width), lambda i: (0, i, 0, 0)), whole(weight), whole(live)],
        [
            ((4, R, MID), F32, (1, R, MID), lambda i: (i, 0, 0)),
            ((nb, 1, 2 * MID), F32, (nb, 1, 2 * MID), lambda i: (0, 0, 0)),
        ],
        [pltpu.VMEM((2, 8, MID), F32)],
        flops=2 * 4 * R * cin * MID,
        moved=4 * R * (2 * cin + 4 * MID) + 2 * cin * MID,
    )


def stage_skip(slabs, weight, live, nb):
    nch, width = slabs.shape[0], slabs.shape[3]
    cin = nch * width

    def body(x_ref, w_ref, live_ref, o_ref, s_ref):
        x = jnp.concatenate([x_ref[k, 0] for k in range(nch)], axis=1)
        value = dot(x, w_ref[0])
        o_ref[...] = value
        value_sums(s_ref, [value[band] for band in bands()], live_ref[...])

    return call(
        body,
        (Q,),
        [
            (slabs, (nch, 1, R, width), lambda i: (0, 0, 0, 0)),
            (weight, (1, cin, MID), lambda i: (i, 0, 0)),
            whole(live),
        ],
        [
            ((R, Q * MID), F32, (R, MID), lambda i: (0, i)),
            ((nb, 1, Q * 2 * MID), F32, (nb, 1, 2 * MID), lambda i: (0, 0, i)),
        ],
        flops=2 * R * cin * Q * MID,
        moved=2 * R * cin + Q * MID * (2 * cin + 4 * R),
    )


def stage_conv_one(conv_a, sums_a, affine, inner, live, kernel, table, nb):
    def body(t_ref, a_ref, s_ref, g_ref, inner_ref, live_ref, k_ref, cols_ref, b_ref, o_ref, pad, acc):
        i = pl.program_id(0)

        @pl.when(i == 0)
        def _():
            scale, shift, _, _ = forward_coef(s_ref[...], g_ref[...], inner_ref[...], t_ref[0])
            pad[1, :, 0] = jnp.zeros((2, 8, 8, MID), F32)
            pad[:, 1, :, 0] = jnp.zeros((2, 8, 8, MID), F32)
            for p in range(4):
                for h, band in enumerate(bands()):
                    u = tall(a_ref[p, band]) * scale + shift
                    pad[p // 2, p % 2, h + 1, 1:8] = silu(u)

        hp = jnp.where(i == 1, 0, 1)
        h0 = jnp.minimum(i, 1)
        taps = []
        for dw in range(3):
            wp = 0 if dw == 1 else 1
            w0 = 0 if dw == 0 else 1
            tap = pad[hp, wp, pl.ds(h0, 7), w0 : w0 + 7].reshape(R, MID).astype(BF)
            cols_ref[:, dw * MID : (dw + 1) * MID] = tap
            taps.append(tap)
        value = sum(dot(taps[dw], jnp.concatenate([k_ref[j, dw] for j in range(Q)], axis=1)) for dw in range(3))

        @pl.when(i == 0)
        def _():
            acc[...] = value

        @pl.when(i > 0)
        def _():
            acc[...] += value

        @pl.when(i == 2)
        def _():
            low = acc[...].astype(BF).astype(F32)
            b_ref[...] = low
            value_sums(o_ref, [low[band] for band in bands()], live_ref[...])

    return call(
        body,
        (3,),
        [
            (table, None),
            whole(conv_a),
            whole(sums_a),
            whole(affine),
            whole(inner),
            whole(live),
            (kernel, (Q, 3, MID, MID // Q), lambda i: (0, i, 0, 0)),
        ],
        [
            ((R, 9 * MID), BF, (R, 3 * MID), lambda i: (0, i)),
            ((R, MID), F32, (R, MID), lambda i: (0, 0)),
            ((nb, 1, 2 * MID), F32, (nb, 1, 2 * MID), lambda i: (0, 0, 0)),
        ],
        [pltpu.VMEM((2, 2, 8, 8, 8, MID), F32), pltpu.VMEM((R, MID), F32)],
        flops=2 * R * 9 * MID * MID,
        moved=4 * 4 * R * MID + 2 * R * 9 * MID + 2 * 9 * MID * MID,
    )


def stage_conv_two(conv_d, sums_d, affine, inner, live, kernel, table, nb):
    def body(t_ref, d_ref, s_ref, g_ref, inner_ref, live_ref, k_ref, cols_ref, e_ref, o_ref, pad, acc):
        i = pl.program_id(0)

        @pl.when(i == 0)
        def _():
            scale, shift, _, _ = forward_coef(s_ref[...], g_ref[...], inner_ref[...], t_ref[1])
            pad[...] = jnp.zeros_like(pad)
            for h, band in enumerate(bands()):
                u = tall(d_ref[band]) * scale + shift
                pad[h + 1, 1:8] = silu(u)

        taps = []
        for dw in range(3):
            tap = pad[pl.ds(i, 7), dw : dw + 7].reshape(R, MID).astype(BF)
            cols_ref[:, dw * MID : (dw + 1) * MID] = tap
            taps.append(tap)
        value = sum(dot(taps[dw], jnp.concatenate([k_ref[j, dw] for j in range(Q)], axis=1)) for dw in range(3))

        @pl.when(i == 0)
        def _():
            acc[...] = value

        @pl.when(i > 0)
        def _():
            acc[...] += value

        @pl.when(i == 2)
        def _():
            low = acc[...].astype(BF).astype(F32)
            e_ref[...] = low
            value_sums(o_ref, [low[band] for band in bands()], live_ref[...])

    return call(
        body,
        (3,),
        [
            (table, None),
            whole(conv_d),
            whole(sums_d),
            whole(affine),
            whole(inner),
            whole(live),
            (kernel, (Q, 3, MID, MID // Q), lambda i: (0, i, 0, 0)),
        ],
        [
            ((R, 9 * MID), BF, (R, 3 * MID), lambda i: (0, i)),
            ((R, MID), F32, (R, MID), lambda i: (0, 0)),
            ((nb, 1, 2 * MID), F32, (nb, 1, 2 * MID), lambda i: (0, 0, 0)),
        ],
        [pltpu.VMEM((9, 9, 8, MID), F32), pltpu.VMEM((R, MID), F32)],
        flops=2 * R * 9 * MID * MID,
        moved=4 * R * MID + 2 * R * 9 * MID + 2 * 9 * MID * MID,
    )


def stage_expand(conv, sums, affine, inner, live, weight, table, nb):
    def body(t_ref, b_ref, s_ref, g_ref, inner_ref, live_ref, w_ref, act_ref, o_ref, sum_ref, wide):
        i = pl.program_id(0)

        @pl.when(i == 0)
        def _():
            scale, shift, _, _ = forward_coef(s_ref[...], g_ref[...], inner_ref[...], t_ref[1])
            for band in bands():
                u = tall(b_ref[band]) * scale + shift
                wide[band] = silu(u).reshape(56, MID)
            act_ref[...] = wide[...].astype(BF)

        value = dot(act_ref[...], w_ref[0])
        o_ref[...] = value
        value_sums(sum_ref, [value[band] for band in bands()], live_ref[...])

    return call(
        body,
        (Q,),
        [
            (table, None),
            whole(conv),
            whole(sums),
            whole(affine),
            whole(inner),
            whole(live),
            (weight, (1, MID, MID), lambda i: (i, 0, 0)),
        ],
        [
            ((R, MID), BF, (R, MID), lambda i: (0, 0)),
            ((R, Q * MID), F32, (R, MID), lambda i: (0, i)),
            ((nb, 1, Q * 2 * MID), F32, (nb, 1, 2 * MID), lambda i: (0, 0, i)),
        ],
        [pltpu.VMEM((R, MID), F32)],
        flops=2 * R * MID * Q * MID,
        moved=4 * R * MID * (Q + 1) + 2 * MID * MID * Q,
    )


def chunk(array, parts=1):
    return (array, (array.shape[0], parts * MID), lambda i: (0, i))


def sum_chunk(array, parts=2):
    return (array, (array.shape[0], 1, parts * MID), lambda i: (0, 0, i))


def stage_join(conv_c, sums_c, affine_c, conv_s, sums_s, affine_s, live, weight, table, nb):
    def body(t_ref, c_ref, sc_ref, gc_ref, v_ref, sv_ref, gv_ref, live_ref, w_ref, f_ref, low_ref, d_ref, o_ref, acc):
        i = pl.program_id(0)
        live = live_ref[...]
        scale_c, shift_c, _, _ = forward_coef(sc_ref[...], gc_ref[...], live, t_ref[1])
        scale_s, shift_s, _, _ = forward_coef(sv_ref[...], gv_ref[...], live, t_ref[1])
        shift = shift_c + shift_s
        for band in bands():
            u = tall(c_ref[band]) * scale_c + tall(v_ref[band]) * scale_s + shift
            f_ref[band] = silu(u).reshape(56, MID)
        low = f_ref[...].astype(BF)
        low_ref[...] = low
        value = dot(low, lanes(w_ref))

        @pl.when(i == 0)
        def _():
            acc[...] = value

        @pl.when(i > 0)
        def _():
            acc[...] += value

        @pl.when(i == Q - 1)
        def _():
            total = acc[...]
            d_ref[...] = total
            value_sums(o_ref, [total[band] for band in bands()], live)

    return call(
        body,
        (Q,),
        [
            (table, None),
            chunk(conv_c),
            sum_chunk(sums_c),
            chunk(affine_c),
            chunk(conv_s),
            sum_chunk(sums_s),
            chunk(affine_s),
            whole(live),
            (weight, (Q, MID, MID // Q), lambda i: (0, i, 0)),
        ],
        [
            ((R, Q * MID), F32, (R, MID), lambda i: (0, i)),
            ((R, Q * MID), BF, (R, MID), lambda i: (0, i)),
            ((R, MID), F32, (R, MID), lambda i: (0, 0)),
            ((nb, 1, 2 * MID), F32, (nb, 1, 2 * MID), lambda i: (0, 0, 0)),
        ],
        [pltpu.VMEM((R, MID), F32)],
        flops=2 * R * MID * Q * MID,
        moved=14 * R * MID * Q + 2 * MID * MID * Q,
    )


def stage_result(conv_f, sums_f, affine, first, cotangent, live, table, nb):
    nch, width = cotangent.shape[0], cotangent.shape[2]
    per = nch // Q

    def body(t_ref, f_ref, s_ref, g_ref, y_ref, ct_ref, live_ref, r_ref, gs_ref, o_ref, wide):
        live = live_ref[...]
        on = t_ref[2]
        scale, shift, mean, inv = forward_coef(s_ref[...], g_ref[...], live, t_ref[1])
        ct = jnp.concatenate([ct_ref[k] for k in range(per)], axis=1).astype(F32)
        first_sum = jnp.zeros((8, MID), F32)
        second_sum = jnp.zeros((8, MID), F32)
        for band in bands():
            v = tall(f_ref[band])
            y = tall(y_ref[band])
            u = v * scale + shift + y
            second, slope = silu_both(u)
            wide[band] = (y + on * (second - y)).reshape(56, MID)
            grad = on * tall(ct[band]) * slope
            gs_ref[band] = grad.reshape(56, MID)
            first_sum = first_sum + jnp.sum(grad, axis=0)
            second_sum = second_sum + jnp.sum(grad * (v - mean), axis=0)
        result = wide[...].astype(BF)
        for k in range(per):
            r_ref[k] = result[:, k * width : (k + 1) * width]
        put_sums(o_ref, [first_sum * live, second_sum * live * inv])

    return call(
        body,
        (Q,),
        [
            (table, None),
            chunk(conv_f),
            sum_chunk(sums_f),
            chunk(affine),
            chunk(first),
            (cotangent, (per, R, width), lambda i: (i, 0, 0)),
            whole(live),
        ],
        [
            ((nch, R, width), BF, (per, R, width), lambda i: (i, 0, 0)),
            ((R, Q * MID), F32, (R, MID), lambda i: (0, i)),
            ((nb, 1, Q * 2 * MID), F32, (nb, 1, 2 * MID), lambda i: (0, 0, i)),
        ],
        [pltpu.VMEM((R, MID), F32)],
        moved=16 * R * Q * MID,
    )


def finish_inner(grad, conv_ref, sums, affine, mask, pixels, out_put, sum_ref):
    scale, shift, mean, inv = forward_coef(sums, affine, mask, pixels)
    first = jnp.zeros((8, MID), F32)
    second = jnp.zeros((8, MID), F32)
    for band in bands():
        v = tall(conv_ref[band])
        gy = mask * (tall(grad[band]) * silu_slope(v * scale + shift))
        out_put(band, gy.reshape(56, MID))
        first = first + jnp.sum(gy, axis=0)
        second = second + jnp.sum(gy * (v - mean), axis=0)
    put_sums(sum_ref, [first, second * inv])


def stage_back_f(gs, conv_f, sums_f, grad_f, affine_f, live, weight, conv_e, sums_e, affine_e, inner, table, nb):
    def body(
        t_ref, gs_ref, f_ref, sf_ref, gf_ref, af_ref, live_ref, w_ref, e_ref, se_ref, ae_ref, inner_ref,
        low_ref, gy_ref, o_ref, acc, wide,
    ):
        i = pl.program_id(0)
        a, b, c = backward_coef(sf_ref[...], gf_ref[...], 1, af_ref[...], live_ref[...], t_ref[1])
        for band in bands():
            wide[band] = (tall(gs_ref[band]) * a + tall(f_ref[band]) * b + c).reshape(56, MID)
        low = wide[...].astype(BF)
        low_ref[...] = low
        value = dot(low, w_ref[0], NT)

        @pl.when(i == 0)
        def _():
            acc[...] = value

        @pl.when(i > 0)
        def _():
            acc[...] += value

        @pl.when(i == Q - 1)
        def _():
            def put(band, piece):
                gy_ref[band] = piece

            finish_inner(acc, e_ref, se_ref[...], ae_ref[...], inner_ref[...], t_ref[1], put, o_ref)

    return call(
        body,
        (Q,),
        [
            (table, None),
            chunk(gs),
            chunk(conv_f),
            sum_chunk(sums_f),
            sum_chunk(grad_f),
            chunk(affine_f),
            whole(live),
            (weight, (1, MID, MID), lambda i: (i, 0, 0)),
            whole(conv_e),
            whole(sums_e),
            whole(affine_e),
            whole(inner),
        ],
        [
            ((R, Q * MID), BF, (R, MID), lambda i: (0, i)),
            ((R, MID), F32, (R, MID), lambda i: (0, 0)),
            ((nb, 1, 2 * MID), F32, (nb, 1, 2 * MID), lambda i: (0, 0, 0)),
        ],
        [pltpu.VMEM((R, MID), F32), pltpu.VMEM((R, MID), F32)],
        flops=2 * R * MID * Q * MID,
        moved=10 * R * MID * Q + 2 * MID * MID * Q,
    )


def stage_back_two(gy_e, conv_e, sums_e, grad_e, affine_e, kernel, conv_d, sums_d, affine_d, inner, table, nb):
    def body(
        t_ref, gy_ref, e_ref, se_ref, ge_ref, ae_ref, k_ref, d_ref, sd_ref, ad_ref, inner_ref,
        low_ref, out_ref, o_ref, pad, acc, wide,
    ):
        i = pl.program_id(0)

        @pl.when(i == 0)
        def _():
            a, b, c = backward_coef(se_ref[...], ge_ref[...], 1, ae_ref[...], inner_ref[...], t_ref[1])
            pad[...] = jnp.zeros_like(pad)
            for h, band in enumerate(bands()):
                value = tall(gy_ref[band]) * a + tall(e_ref[band]) * b + c
                wide[band] = value.reshape(56, MID)
                pad[h + 1, 1:8] = value
            low_ref[...] = wide[...].astype(BF)

        total = None
        for dw in range(3):
            tap = pad[pl.ds(2 - i, 7), 2 - dw : 9 - dw].reshape(R, MID).astype(BF)
            part = dot(tap, jnp.concatenate([k_ref[j, dw] for j in range(Q)], axis=1), NT)
            total = part if total is None else total + part

        @pl.when(i == 0)
        def _():
            acc[...] = total

        @pl.when(i > 0)
        def _():
            acc[...] += total

        @pl.when(i == 2)
        def _():
            low = acc[...].astype(BF).astype(F32)

            def put(band, piece):
                out_ref[band] = piece

            finish_inner(low, d_ref, sd_ref[...], ad_ref[...], inner_ref[...], t_ref[1], put, o_ref)

    return call(
        body,
        (3,),
        [
            (table, None),
            whole(gy_e),
            whole(conv_e),
            whole(sums_e),
            whole(grad_e),
            whole(affine_e),
            (kernel, (Q, 3, MID, MID // Q), lambda i: (0, i, 0, 0)),
            whole(conv_d),
            whole(sums_d),
            whole(affine_d),
            whole(inner),
        ],
        [
            ((R, MID), BF, (R, MID), lambda i: (0, 0)),
            ((R, MID), F32, (R, MID), lambda i: (0, 0)),
            ((nb, 1, 2 * MID), F32, (nb, 1, 2 * MID), lambda i: (0, 0, 0)),
        ],
        [pltpu.VMEM((9, 9, 8, MID), F32), pltpu.VMEM((R, MID), F32), pltpu.VMEM((R, MID), F32)],
        flops=2 * R * 9 * MID * MID,
        moved=16 * R * MID + 2 * 9 * MID * MID,
    )


def stage_back_join(
    gy_d, conv_d, sums_d, grad_d, affine_d, inner, weight, cotangent, gs, conv_c, sums_c, affine_c, conv_s, sums_s,
    affine_s, live, table, nb,
):
    nch, width = cotangent.shape[0], cotangent.shape[2]
    per = nch // Q

    def body(
        t_ref, gy_ref, d_ref, sd_ref, gd_ref, ad_ref, inner_ref, w_ref, ct_ref, gs_ref, c_ref, sc_ref, ac_ref, v_ref,
        sv_ref, av_ref, live_ref, low_ref, out_ref, o_ref, wide,
    ):
        i = pl.program_id(0)
        live = live_ref[...]

        @pl.when(i == 0)
        def _():
            a, b, c = backward_coef(sd_ref[...], gd_ref[...], 1, ad_ref[...], inner_ref[...], t_ref[1])
            for band in bands():
                wide[band] = (tall(gy_ref[band]) * a + tall(d_ref[band]) * b + c).reshape(56, MID)
            low_ref[...] = wide[...].astype(BF)

        back = dot(low_ref[...], lanes(w_ref), NT)
        ct = jnp.concatenate([ct_ref[k] for k in range(per)], axis=1).astype(F32)
        scale_c, shift_c, mean_c, inv_c = forward_coef(sc_ref[...], ac_ref[...], live, t_ref[1])
        scale_s, shift_s, mean_s, inv_s = forward_coef(sv_ref[...], av_ref[...], live, t_ref[1])
        shift = shift_c + shift_s
        off = 1.0 - t_ref[2]
        one = jnp.zeros((8, MID), F32)
        two = jnp.zeros((8, MID), F32)
        three = jnp.zeros((8, MID), F32)
        for band in bands():
            c = tall(c_ref[band])
            v = tall(v_ref[band])
            u = c * scale_c + v * scale_s + shift
            grad = off * tall(ct[band]) + tall(gs_ref[band]) + tall(back[band])
            grad = live * (grad * silu_slope(u))
            out_ref[band] = grad.reshape(56, MID)
            one = one + jnp.sum(grad, axis=0)
            two = two + jnp.sum(grad * (c - mean_c), axis=0)
            three = three + jnp.sum(grad * (v - mean_s), axis=0)
        put_sums(o_ref, [one, two * inv_c, three * inv_s])

    return call(
        body,
        (Q,),
        [
            (table, None),
            whole(gy_d),
            whole(conv_d),
            whole(sums_d),
            whole(grad_d),
            whole(affine_d),
            whole(inner),
            (weight, (Q, MID, MID // Q), lambda i: (0, i, 0)),
            (cotangent, (per, R, width), lambda i: (i, 0, 0)),
            chunk(gs),
            chunk(conv_c),
            sum_chunk(sums_c),
            chunk(affine_c),
            chunk(conv_s),
            sum_chunk(sums_s),
            chunk(affine_s),
            whole(live),
        ],
        [
            ((R, MID), BF, (R, MID), lambda i: (0, 0)),
            ((R, Q * MID), F32, (R, MID), lambda i: (0, i)),
            ((nb, 1, Q * 3 * MID), F32, (nb, 1, 3 * MID), lambda i: (0, 0, i)),
        ],
        [pltpu.VMEM((R, MID), F32)],
        flops=2 * R * MID * Q * MID,
        moved=18 * R * MID * Q + 2 * MID * MID * Q,
    )


def stage_back_first(
    grad, sums_g, conv_c, sums_c, affine_c, conv_s, sums_s, affine_s, live, weight, conv_b, sums_b, affine_b, inner,
    table, nb,
):
    def body(
        t_ref, g_ref, sg_ref, c_ref, sc_ref, ac_ref, v_ref, sv_ref, av_ref, live_ref, w_ref, b_ref, sb_ref, ab_ref,
        inner_ref, lowc_ref, lows_ref, out_ref, o_ref, acc, wide,
    ):
        i = pl.program_id(0)
        live = live_ref[...]
        a, b, c = backward_coef(sv_ref[...], sg_ref[...], 2, av_ref[...], live, t_ref[1])
        for band in bands():
            wide[band] = (tall(g_ref[band]) * a + tall(v_ref[band]) * b + c).reshape(56, MID)
        lows_ref[...] = wide[...].astype(BF)
        a, b, c = backward_coef(sc_ref[...], sg_ref[...], 1, ac_ref[...], live, t_ref[1])
        for band in bands():
            wide[band] = (tall(g_ref[band]) * a + tall(c_ref[band]) * b + c).reshape(56, MID)
        low = wide[...].astype(BF)
        lowc_ref[...] = low
        value = dot(low, w_ref[0], NT)

        @pl.when(i == 0)
        def _():
            acc[...] = value

        @pl.when(i > 0)
        def _():
            acc[...] += value

        @pl.when(i == Q - 1)
        def _():
            def put(band, piece):
                out_ref[band] = piece

            finish_inner(acc, b_ref, sb_ref[...], ab_ref[...], inner_ref[...], t_ref[1], put, o_ref)

    return call(
        body,
        (Q,),
        [
            (table, None),
            chunk(grad),
            sum_chunk(sums_g, 3),
            chunk(conv_c),
            sum_chunk(sums_c),
            chunk(affine_c),
            chunk(conv_s),
            sum_chunk(sums_s),
            chunk(affine_s),
            whole(live),
            (weight, (1, MID, MID), lambda i: (i, 0, 0)),
            whole(conv_b),
            whole(sums_b),
            whole(affine_b),
            whole(inner),
        ],
        [
            ((R, Q * MID), BF, (R, MID), lambda i: (0, i)),
            ((R, Q * MID), BF, (R, MID), lambda i: (0, i)),
            ((R, MID), F32, (R, MID), lambda i: (0, 0)),
            ((nb, 1, 2 * MID), F32, (nb, 1, 2 * MID), lambda i: (0, 0, 0)),
        ],
        [pltpu.VMEM((R, MID), F32), pltpu.VMEM((R, MID), F32)],
        flops=2 * R * MID * Q * MID,
        moved=16 * R * MID * Q + 2 * MID * MID * Q,
    )


def stage_back_skip(low, weight):
    cin = weight.shape[1]

    def body(g_ref, w_ref, o_ref):
        i = pl.program_id(0)
        value = dot(g_ref[...], w_ref[0], NT)

        @pl.when(i == 0)
        def _():
            o_ref[...] = value

        @pl.when(i > 0)
        def _():
            o_ref[...] += value

    return call(
        body,
        (Q,),
        [chunk(low), (weight, (1, cin, MID), lambda i: (i, 0, 0))],
        [((R, cin), F32, (R, cin), lambda i: (0, 0))],
        flops=2 * R * cin * Q * MID,
        moved=4 * R * cin + 2 * R * Q * MID + 2 * cin * Q * MID,
    )[0]


def stage_back_one(gy_b, conv_b, sums_b, grad_b, affine_b, kernel, conv_a, sums_a, affine_a, inner, table, nb):
    def body(
        t_ref, gy_ref, b_ref, sb_ref, gb_ref, ab_ref, k_ref, a_ref, sa_ref, aa_ref, inner_ref,
        low_ref, out_ref, o_ref, pad, acc, wide,
    ):
        i = pl.program_id(0)

        @pl.when(i == 0)
        def _():
            a, b, c = backward_coef(sb_ref[...], gb_ref[...], 1, ab_ref[...], inner_ref[...], t_ref[1])
            pad[7] = jnp.zeros((8, 8, MID), F32)
            pad[:, 7] = jnp.zeros((8, 8, MID), F32)
            for h, band in enumerate(bands()):
                value = tall(gy_ref[band]) * a + tall(b_ref[band]) * b + c
                wide[band] = value.reshape(56, MID)
                pad[h, 0:7] = value
            low_ref[...] = wide[...].astype(BF)

        h0 = jnp.where(i == 0, 1, 0)
        near = pad[pl.ds(h0, 7), 0:7].reshape(R, MID).astype(BF)
        far = pad[pl.ds(h0, 7), 1:8].reshape(R, MID).astype(BF)
        k = [jnp.concatenate([k_ref[j, dw] for j in range(Q)], axis=1) for dw in range(3)]
        even = dot(near, k[1], NT)
        odd = dot(far, k[0], NT) + dot(near, k[2], NT)

        @pl.when(i == 0)
        def _():
            acc[2] = even
            acc[3] = odd

        @pl.when(i == 1)
        def _():
            acc[0] = even
            acc[1] = odd

        @pl.when(i == 2)
        def _():
            acc[2] += even
            acc[3] += odd
            mask = inner_ref[...]
            scale, shift, mean, inv = forward_coef(sa_ref[...], aa_ref[...], mask, t_ref[0])
            first = jnp.zeros((8, MID), F32)
            second = jnp.zeros((8, MID), F32)
            for p in range(4):
                wide[...] = acc[p].astype(BF).astype(F32)
                for band in bands():
                    v = tall(a_ref[p, band])
                    gy = mask * (tall(wide[band]) * silu_slope(v * scale + shift))
                    out_ref[p, band] = gy.reshape(56, MID)
                    first = first + jnp.sum(gy, axis=0)
                    second = second + jnp.sum(gy * (v - mean), axis=0)
            put_sums(o_ref, [first, second * inv])

    return call(
        body,
        (3,),
        [
            (table, None),
            whole(gy_b),
            whole(conv_b),
            whole(sums_b),
            whole(grad_b),
            whole(affine_b),
            (kernel, (Q, 3, MID, MID // Q), lambda i: (0, i, 0, 0)),
            whole(conv_a),
            whole(sums_a),
            whole(affine_a),
            whole(inner),
        ],
        [
            ((R, MID), BF, (R, MID), lambda i: (0, 0)),
            ((4, R, MID), F32, (4, R, MID), lambda i: (0, 0, 0)),
            ((nb, 1, 2 * MID), F32, (nb, 1, 2 * MID), lambda i: (0, 0, 0)),
        ],
        [pltpu.VMEM((8, 8, 8, MID), F32), pltpu.VMEM((4, R, MID), F32), pltpu.VMEM((R, MID), F32)],
        flops=2 * R * 9 * MID * MID,
        moved=32 * R * MID + 2 * 9 * MID * MID,
    )


def stage_back_in(gy_a, conv_a, sums_a, grad_a, affine_a, weight, skip_grad, inner, table, nch):
    cin = weight.shape[1]
    width = cin // nch

    def body(t_ref, gy_ref, a_ref, sa_ref, ga_ref, aa_ref, w_ref, s_ref, inner_ref, low_ref, out_ref, wide):
        i = pl.program_id(0)
        a, b, c = backward_coef(sa_ref[...], ga_ref[...], 1, aa_ref[...], inner_ref[...], t_ref[0])
        for band in bands():
            wide[band] = (tall(gy_ref[0, band]) * a + tall(a_ref[0, band]) * b + c).reshape(56, MID)
        low = wide[...].astype(BF)
        low_ref[0] = low
        value = dot(low, lanes(w_ref), NT)

        @pl.when(i == 0)
        def _():
            both = (value + s_ref[...]).astype(BF)
            for k in range(nch):
                out_ref[k, 0] = both[:, k * width : (k + 1) * width]

        @pl.when(i > 0)
        def _():
            both = value.astype(BF)
            for k in range(nch):
                out_ref[k, 0] = both[:, k * width : (k + 1) * width]

    return call(
        body,
        (4,),
        [
            (table, None),
            (gy_a, (1, R, MID), lambda i: (i, 0, 0)),
            (conv_a, (1, R, MID), lambda i: (i, 0, 0)),
            whole(sums_a),
            whole(grad_a),
            whole(affine_a),
            whole(weight),
            whole(skip_grad),
            whole(inner),
        ],
        [
            ((4, R, MID), BF, (1, R, MID), lambda i: (i, 0, 0)),
            ((nch, 4, R, width), BF, (nch, 1, R, width), lambda i: (0, i, 0, 0)),
        ],
        [pltpu.VMEM((R, MID), F32)],
        flops=2 * 4 * R * cin * MID,
        moved=4 * R * (10 * MID + 2 * cin) + 2 * cin * MID + 4 * R * cin,
    )


def after(value, *others):
    return lax.optimization_barrier((value,) + others)[0]


NEAR = [(i, i ^ 1) for i in range(Q)]
FAR = [(i, i ^ 2) for i in range(Q)]


def gather_far(part, nch):
    return lax.ppermute(part, "chan", FAR) if nch == Q else None


def gather_far_slices(parts, nb, nch):
    if nch != Q:
        return [None] * len(parts)
    b = lax.axis_index("batch")
    slices = [lax.dynamic_index_in_dim(part.reshape(nb, -1, part.shape[-1]), b, 0, keepdims=False) for part in parts]
    return [lax.ppermute(piece, "chan", FAR) for piece in slices]


def share(piece, shape, nb):
    got = lax.all_to_all(jnp.broadcast_to(piece[None], (nb,) + piece.shape), "batch", 0, 0)
    return got.reshape(shape)


def gather_rest(part, other, nch):
    if nch == Q:
        c = lax.axis_index("chan")
        parts = [part, lax.ppermute(part, "chan", NEAR), other, lax.ppermute(other, "chan", NEAR)]
        return place(parts, c)
    full = lax.all_gather(part, "chan", axis=part.ndim - 1, tiled=True)
    cut = full.reshape(full.shape[:-1] + (Q, full.shape[-1] // Q))
    return jnp.moveaxis(cut, -2, 0)


def place(parts, c):
    shape = parts[0].shape
    cuts = shape[0] // 3 if len(shape) == 3 else 1
    block = (3,) + shape[1:] if len(shape) == 3 else shape
    rest = (0,) * (len(shape) - 1)

    def body(c_ref, *refs):
        k = pl.program_id(0)
        out = refs[Q]
        for j in range(Q):

            @pl.when(k == j)
            def _():
                out[0] = refs[j][...]

    def spec(j):
        def index(k, i, c_ref):
            return (jnp.where(k == j, i, jnp.where(k < j, 0, cuts - 1)),) + rest

        return pl.BlockSpec(block, index)

    grid_spec = pltpu.PrefetchScalarGridSpec(
        num_scalar_prefetch=1,
        grid=(Q, cuts),
        in_specs=[spec(j) for j in range(Q)],
        out_specs=pl.BlockSpec((1,) + block, lambda k, i, c_ref: (jnp.bitwise_xor(c_ref[0], k), i) + rest),
    )
    return pl.pallas_call(
        body,
        grid_spec=grid_spec,
        out_shape=jax.ShapeDtypeStruct((Q,) + shape, parts[0].dtype),
        compiler_params=pltpu.CompilerParams(vmem_limit_bytes=VMEM_LIMIT),
        cost_estimate=pl.CostEstimate(flops=0, bytes_accessed=4 * Q * parts[0].size, transcendentals=0),
    )(c.reshape(1).astype(jnp.int32), *parts)


def to_subnets(blocks, groups):
    if groups > 1:
        images = 8 // groups
        shape = blocks.shape
        cut = blocks.reshape(shape[:-2] + (49, groups, images, shape[-1]))
        cut = jnp.moveaxis(cut, -3, 1)
        cut = jnp.pad(cut, [(0, 0)] * (cut.ndim - 2) + [(0, 8 - images), (0, 0)])
        blocks = cut.reshape((shape[0] * groups,) + shape[1:])
    return lax.all_to_all(blocks, "chan", 0, 0)


def from_subnets(blocks, groups):
    back = lax.all_to_all(blocks, "chan", 0, 0)
    if groups > 1:
        images = 8 // groups
        shape = back.shape
        cut = back.reshape((shape[0] // groups, groups) + shape[1:-2] + (49, 8, shape[-1]))[..., :images, :]
        cut = jnp.moveaxis(cut, 1, -3)
        back = cut.reshape((shape[0] // groups,) + shape[1:-2] + (R, shape[-1]))
    return back


def make_sync(groups, nch):
    def sync(sums):
        got = lax.all_to_all(sums, "batch", 0, 0)
        if groups > 1:
            pairs = [[g * groups + k for k in range(groups)] for g in range(nch // groups)]
            got = lax.psum(got, "chan", axis_index_groups=pairs)
        return got

    return sync


def weight_product(left, grad, columns, plus, width, apart):
    phases, rows = grad.shape[0], grad.shape[1]
    if left.ndim == 2:
        depth = left.shape[1]
        step = {4608: 1536, 2048: 1024}.get(depth, 512)
        left_spec = pl.BlockSpec((rows, step), lambda i, c: (0, i))
    else:
        step = left.shape[3]
        depth = left.shape[0] * step
        left_spec = pl.BlockSpec((1, phases, rows, step), lambda i, c: (i, 0, 0, 0))
    flat = left.ndim == 2

    def body(c_ref, l_ref, one_ref, two_ref, *refs):
        value = None
        for p in range(phases):
            piece = dot(
                l_ref[...] if flat else l_ref[0, p], jnp.concatenate([one_ref[p], two_ref[p]], axis=1), TN
            )
            value = piece if value is None else value + piece
        halves = [value[:, :width], value[:, width:]]
        outs = refs
        if plus is not None:
            halves = [halves[k] + refs[0][k].astype(F32) for k in range(2)]
            outs = refs[1:]
        for k in range(2):
            if apart:
                outs[k][...] = halves[k].astype(BF)
            else:
                outs[0][k] = halves[k].astype(BF)

    def grad_spec(k):
        return pl.BlockSpec((phases, rows, width), lambda i, c: (0, 0, c[k]))

    pair = pl.BlockSpec((2, step, width), lambda i, c: (0, i, 0))
    single = pl.BlockSpec((step, width), lambda i, c: (i, 0))
    grid_spec = pltpu.PrefetchScalarGridSpec(
        num_scalar_prefetch=1,
        grid=(depth // step,),
        in_specs=[left_spec, grad_spec(0), grad_spec(1)] + ([] if plus is None else [pair]),
        out_specs=[single, single] if apart else pair,
    )
    one = jax.ShapeDtypeStruct((depth, width), BF)
    return pl.pallas_call(
        body,
        grid_spec=grid_spec,
        out_shape=[one, one] if apart else jax.ShapeDtypeStruct((2, depth, width), BF),
        compiler_params=pltpu.CompilerParams(vmem_limit_bytes=VMEM_LIMIT),
        cost_estimate=pl.CostEstimate(
            flops=4 * phases * rows * depth * width,
            bytes_accessed=2 * (phases * rows * (depth + 2 * width) + 4 * depth * width),
            transcendentals=0,
        ),
    )(columns, left, grad, grad, *([] if plus is None else [plus]))


class Reduce:
    def __init__(self, nb, nch, left, grad, lead=()):
        self.nb, self.nch, self.left, self.lead = nb, nch, left, lead
        self.grad = grad if grad.ndim == 3 else grad[None]
        self.width = self.grad.shape[2] // nch
        self.depth = left.shape[1] if left.ndim == 2 else left.shape[0] * left.shape[3]
        self.quick = nch == Q

    def first(self):
        if not self.quick:
            left = self.left
            if left.ndim == 4:
                left = jnp.transpose(left[:, : self.grad.shape[0]], (1, 2, 0, 3)).reshape(-1, self.depth)
            full = dot(left, self.grad.reshape(-1, self.grad.shape[2]), TN).astype(BF)
            self.value = lax.psum_scatter(full, "chan", scatter_dimension=1, tiled=True)
            return []
        c = lax.axis_index("chan").astype(jnp.int32)
        self.value = weight_product(self.left, self.grad, jnp.stack([c ^ 1, c ^ 3]), None, self.width, False)
        return [self.value]

    def near(self, held=None):
        if self.quick:
            self.value = lax.ppermute(held[0], "chan", NEAR)

    def second(self):
        if not self.quick:
            return []
        c = lax.axis_index("chan").astype(jnp.int32)
        out = weight_product(self.left, self.grad, jnp.stack([c, c ^ 2]), self.value, self.width, True)
        return list(out)

    def far(self, held=None):
        if self.quick:
            self.own = held[0]
            self.value = lax.ppermute(held[1], "chan", FAR)

    def third(self):
        part = self.value
        if self.quick:
            part = (self.own.astype(F32) + self.value.astype(F32)).astype(BF)
        if self.lead:
            part = jnp.moveaxis(part.reshape(self.lead + (self.nb, -1, self.width)), len(self.lead), 0)
        else:
            part = part.reshape(self.nb, self.depth // self.nb, self.width)
        return [part]

    def batch(self, held):
        self.value = lax.all_to_all(held[0], "batch", 0, 0)

    def total(self):
        return jnp.sum(self.value.astype(F32), axis=0)


def slot(value, *groups):
    flat = [array for group in groups for array in group]
    held = lax.optimization_barrier((value, *flat))
    out = []
    at = 1
    for group in groups:
        out.append(list(held[at : at + len(group)]))
        at += len(group)
    return [held[0]] + out


def body(
    inputs, weight_in, kernel_one, weight_out, weight_skip, second_in, kernel_two, second_out, norm_reduce,
    norm_kernel, norm_expand, norm_skip, later_reduce, later_kernel, later_expand, widths, depths, counts, cotangent,
    *, nb, nch,
):
    subnets, per = inputs.shape[0], inputs.shape[1]
    groups = nch // subnets
    images = per // groups
    chan = lax.axis_index("chan")
    member, half = chan // groups, chan % groups
    slots = jnp.arange(8, dtype=jnp.int32)
    ids = lax.axis_index("batch") * per + half * images + slots
    count = counts[member]
    live_image = jnp.logical_and(slots < images, ids < count).astype(F32)[:, None]
    live = jnp.broadcast_to(live_image, (8, MID))
    inner = live * (jnp.arange(MID, dtype=jnp.int32) < widths[member]).astype(F32)[None, :]
    high, low = inputs.shape[2], cotangent.shape[2]
    table = jnp.stack(
        [
            count.astype(F32) * (high * high),
            count.astype(F32) * (low * low),
            (depths[member] == 2).astype(F32),
        ]
    )
    sync = make_sync(groups, nch)

    small = (norm_reduce, norm_kernel, later_reduce, later_kernel)
    large = (norm_expand, norm_skip, later_expand)
    joined = jnp.concatenate(small + large, axis=1)
    spread = lax.all_to_all(jnp.broadcast_to(joined[None], (nch,) + joined.shape), "chan", 0, 0)
    at = 0
    full = []
    for part in small + large:
        piece = lax.slice_in_dim(spread, at, at + part.shape[1], axis=2)
        full.append(jnp.moveaxis(piece, 0, 1).reshape(2, -1))
        at += part.shape[1]
    aff_a, aff_b, aff_d, aff_e, aff_c, aff_s, aff_f = full

    flat_one = kernel_one.reshape((9,) + kernel_one.shape[2:])
    flat_two = kernel_two.reshape((9,) + kernel_two.shape[2:])
    rows = rows_in(inputs)
    far = gather_far(weight_in, nch)
    late = [weight_skip, flat_two, second_out]
    pieces = gather_far_slices(late, nb, nch)
    if nch == Q:
        rows = after(rows, far, *pieces)
    w_in = gather_rest(weight_in, far, nch)
    slabs = to_subnets(rows, groups)
    if nch == Q:
        pieces = [share(piece, part.shape, nb) for piece, part in zip(pieces, late)]
    far_one = gather_far(after(flat_one, slabs), nch)

    conv_a, sums = stage_a(slabs, w_in, live, nb)
    sums_a = sync(sums)
    w_skip = gather_rest(weight_skip, pieces[0], nch)
    sums_a, (w_skip,) = slot(sums_a, [w_skip])
    conv_s, sums = stage_skip(slabs, w_skip, live, nb)
    sums_s = sync(sums)
    k_one = gather_rest(flat_one, far_one, nch)
    far_out = gather_far(after(weight_out, k_one), nch)
    cols_a, conv_b, sums = stage_conv_one(conv_a, sums_a, aff_a, inner, live, k_one, table, nb)
    sums_b = sync(sums)
    w_out = gather_rest(weight_out, far_out, nch)
    far_in = gather_far(after(second_in, w_out), nch)
    act_b, conv_c, sums = stage_expand(conv_b, sums_b, aff_b, inner, live, w_out, table, nb)
    sums_c = sync(sums)
    k_two = gather_rest(flat_two, pieces[1], nch)
    s_in = gather_rest(second_in, far_in, nch)
    sums_c, (s_in,) = slot(sums_c, [s_in])
    first, first_low, conv_d, sums = stage_join(
        conv_c, sums_c, aff_c, conv_s, sums_s, aff_s, live, s_in, table, nb
    )
    cot = to_subnets(after(small_in(cotangent), sums), groups)
    sums_d = sync(sums)
    sums_d, (k_two,) = slot(sums_d, [k_two])
    cols_d, conv_e, sums = stage_conv_two(conv_d, sums_d, aff_d, inner, live, k_two, table, nb)
    sums_e = sync(sums)
    s_out = gather_rest(second_out, pieces[2], nch)
    sums_e, (s_out,) = slot(sums_e, [s_out])
    act_e, conv_f, sums = stage_expand(conv_e, sums_e, aff_e, inner, live, s_out, table, nb)
    sums_f = sync(sums)
    result, grad_sum, sums = stage_result(conv_f, sums_f, aff_f, first, cot, live, table, nb)
    grads_f = sync(sums)
    result = small_out(from_subnets(result, groups), subnets)

    low_f, gy_e, sums = stage_back_f(
        grad_sum, conv_f, sums_f, grads_f, aff_f, live, s_out, conv_e, sums_e, aff_e, inner, table, nb
    )
    grads_e = sync(sums)
    d_sout = Reduce(nb, nch, act_e, low_f)
    grads_e, x = slot(grads_e, d_sout.first())
    d_sout.near(x)
    low_e, gy_d, sums = stage_back_two(
        gy_e, conv_e, sums_e, grads_e, aff_e, k_two, conv_d, sums_d, aff_d, inner, table, nb
    )
    grads_d = sync(sums)
    d_two = Reduce(nb, nch, cols_d, low_e, (9,))
    grads_d, x, y = slot(grads_d, d_sout.second(), d_two.first())
    d_sout.far(x)
    d_two.near(y)
    low_d, grad_one, sums = stage_back_join(
        gy_d, conv_d, sums_d, grads_d, aff_d, inner, s_in, cot, grad_sum, conv_c, sums_c, aff_c, conv_s, sums_s,
        aff_s, live, table, nb,
    )
    grads_j = sync(sums)
    d_sin = Reduce(nb, nch, first_low, low_d)
    grads_j, x, y, z = slot(grads_j, d_sout.third(), d_two.second(), d_sin.first())
    d_sout.batch(x)
    d_two.far(y)
    d_sin.near(z)
    low_c, low_s, gy_b, sums = stage_back_first(
        grad_one, grads_j, conv_c, sums_c, aff_c, conv_s, sums_s, aff_s, live, w_out, conv_b, sums_b, aff_b, inner,
        table, nb,
    )
    grads_b = sync(sums)
    d_out = Reduce(nb, nch, act_b, low_c)
    d_skip = Reduce(nb, nch, slabs, low_s)
    skip_grad = stage_back_skip(low_s, w_skip)
    grads_b, x, y, z = slot(grads_b, d_sin.second(), d_out.first(), d_skip.first())
    d_sin.far(x)
    d_out.near(y)
    d_skip.near(z)
    low_b, gy_a, sums = stage_back_one(
        gy_b, conv_b, sums_b, grads_b, aff_b, k_one, conv_a, sums_a, aff_a, inner, table, nb
    )
    grads_a = sync(sums)
    d_one = Reduce(nb, nch, cols_a, low_b, (9,))
    grads_a, x, y, z, v, w, (skip_grad,) = slot(
        grads_a, d_two.third(), d_sin.third(), d_out.second(), d_skip.second(), d_one.first(), [skip_grad]
    )
    d_two.batch(x)
    d_sin.batch(y)
    d_out.far(z)
    d_skip.far(v)
    d_one.near(w)
    low_a, grad_in = stage_back_in(gy_a, conv_a, sums_a, grads_a, aff_a, w_in, skip_grad, inner, table, nch)
    d_in = Reduce(nb, nch, slabs, low_a)
    inputs_grad = rows_out(from_subnets(grad_in, groups), subnets)
    d_one.far(d_one.second())
    d_out.batch(d_out.third())
    d_skip.batch(d_skip.third())
    d_in.near(d_in.first())
    d_in.far(d_in.second())
    d_one.batch(d_one.third())
    d_in.batch(d_in.third())
    weight_in_grad, kernel_one_grad, weight_out_grad = d_in.total(), d_one.total(), d_out.total()
    weight_skip_grad, second_in_grad = d_skip.total(), d_sin.total()
    kernel_two_grad, second_out_grad = d_two.total(), d_sout.total()

    def pair(sums, parts, which):
        total = jnp.sum(sums, axis=0).reshape(-1, parts, MID)
        both = jnp.stack([total[:, which].reshape(-1), total[:, 0].reshape(-1)])
        return both.reshape(2, nch, -1)

    norm_parts = [
        pair(grads_a, 2, 1), pair(grads_b, 2, 1), pair(grads_j, 3, 1), pair(grads_j, 3, 2), pair(grads_d, 2, 1),
        pair(grads_e, 2, 1), pair(grads_f, 2, 1),
    ]
    joined = jnp.moveaxis(jnp.concatenate(norm_parts, axis=2), 1, 0)
    mine = jnp.sum(lax.all_to_all(joined, "chan", 0, 0), axis=0) / groups
    norm_grads = []
    at = 0
    for part in norm_parts:
        norm_grads.append(mine[:, at : at + part.shape[2]])
        at += part.shape[2]

    shape = (3, 3, MID // nb, MID // nch)
    return (
        result, inputs_grad, weight_in_grad, kernel_one_grad.reshape(shape), weight_out_grad, weight_skip_grad,
        second_in_grad, kernel_two_grad.reshape(shape), second_out_grad, *norm_grads,
    )


def solution(mesh):
    nb, nch = mesh.shape["batch"], mesh.shape["chan"]
    maps = P(None, "batch", None, None, "chan")
    cols = P(None, "chan")
    taps = P(None, None, None, "chan")
    in_specs = (maps, cols, taps, cols, cols, cols, taps, cols) + (cols,) * 7 + (P(), P(), P(), maps)
    both = P("batch", "chan")
    split = P(None, None, "batch", "chan")
    out_specs = (maps, maps, both, split, both, both, both, split, both) + (cols,) * 7

    def run(*args):
        return body(*args, nb=nb, nch=nch)

    return jax.shard_map(run, mesh=mesh, in_specs=in_specs, out_specs=out_specs, check_vma=False)
```

time: 2780 us -> 766 us (0.28)
  local copies, waits for them, and re-layouts: 1030 us -> 110 us
  other arithmetic: 392 us -> 25.2 us
  waiting for transfers between devices: 574 us -> 210 us
  blocking collectives: 367 us -> 111 us
  matrix products: 224 us -> 0 us
  Pallas kernels: 0 us -> 165 us
    unnamed x1264 -> x301, local copies, waits for them, and re-layouts: 512 us -> 85.6 us
    reduce_scatter x13 -> x0, waiting for transfers between devices: 334 us -> none  [the longest x8 204 us: spread_grad(): lax.psum_scatter(partial_sum.astype(jnp.bfloat16), 'chan', scatter_dimens...]
    psum x12 -> x0, blocking collectives: 313 us -> none  [channel_sums(): return lax.psum((first_sum, second_sum), 'batch')]
    slice x92 -> x3, local copies, waits for them, and re-layouts: 246 us -> 1.18 us  [the longest x2 1.18 us: body(): norm_grads.append(mine[:, at:at + part.shape[2]])]
    dot_general x84 -> x0, matrix products: 224 us -> none  [the longest x8 55.8 us: spatial_backward(): jnp.einsum('pk,po->ko', flat_cols, flat_grad, preferred_element_type=jnp....]
    scatter-add x40 -> x0, other arithmetic: 204 us -> none  [the longest x36 166 us: fold_back(): summed = summed.at[:, row_off:row_off + extent:stride, col_off:col_off +...]
    all_gather x10 -> x0, waiting for transfers between devices: 180 us -> none  [the longest x8 180 us: gather_feat(): return lax.all_gather(active, 'chan', axis=4, tiled=True)]
    pallas_call x0 -> x36, Pallas kernels: none -> 165 us  [the longest x15 87.8 us: call(): pl.pallas_call(body, grid=grid, in_specs=in_specs, out_specs=[pl.BlockSpe...]
  transfers between devices with their start and end apart: 67 -> 58, of which waited for: 25 -> 21; matrix products, arithmetic and copies ran while one was open for 54% -> 7% of each run, Pallas kernels for 0% -> 20%
where the time goes in v1:
time: 766 us; the launch traced here: 752 us
  waiting for transfers between devices  210 us (27%)
  Pallas kernels  165 us (22%)
  starting transfers between devices  127 us (17%)
  blocking collectives  111 us (14%)
  local copies, waits for them, and re-layouts  110 us (14%)
  other arithmetic  25.2 us (3%)
    pallas_call x15, Pallas kernels, call(): pl.pallas_call(body, grid=grid, in_specs=in_specs, out_specs=[pl.BlockSpe...  87.8 us
    unnamed x301, local copies, waits for them, and re-layouts  85.6 us
    ppermute x7, waiting for transfers between devices, far(): self.value = lax.ppermute(held[1], 'chan', FAR)  83.9 us
    all_to_all x2, blocking collectives, to_subnets(): return lax.all_to_all(blocks, 'chan', 0, 0)  67.1 us
    all_to_all x6, waiting for transfers between devices, batch(): self.value = lax.all_to_all(held[0], 'batch', 0, 0)  61.9 us
    all_to_all x11, starting transfers between devices, sync(): got = lax.all_to_all(sums, 'batch', 0, 0)  55.5 us
    pallas_call x14, Pallas kernels, weight_product(): pl.pallas_call(body, grid_spec=grid_spec, out_shape=[one, one] if apart e...  49.3 us
    all_to_all x6, starting transfers between devices, batch(): self.value = lax.all_to_all(held[0], 'batch', 0, 0)  27.6 us
  transfers between devices with their start and end apart: 58, of which 21 were waited for; matrix products, arithmetic and copies ran while one was open for 7% of the time, Pallas kernels for 20%

profile of v1, /device:TPU:0, one launch (start us, length us, event | category | flops | bytes accessed | tf_op | source)
XLA Modules:
  0.0 751.5 jit_solution(2739416738820137661)
XLA Ops:
  21.7 43.0 %all_to_all.145.x_ref.l_ref = bf16[4,4,392,256]{3,2,1,0:T(8,128)(2,1)} all-to-all(bf16[4,4,392,256]{3,2,1,0:T(8,128)(2,1)} %bitcast.142), channel_id=1, replica_groups=mesh['batch'=8,'chan'=4] {'chan'}, dimensions={0} | all-to-all | bytes 6422528 | tf_op jit(solution)/shard_map/all_to_all | solution.py:981
  65.8 6.3 all-to-all-start.2
  80.0 17.9 %all-to-all-done.2 = bf16[8,128,512]{2,1,0:T(8,128)(2,1)} async-done(((bf16[8,128,512]{2,1,0:T(8,128)(2,1)}), bf16[8,128,512]{2,1,0:T(8,128)(2,1)}, u32[]{:S(2)}, u32[]{:S(2)}) %all-to-all-start.2) | async-done | bytes 1048608 | tf_op jit(solution)/shard_map/all_to_all | solution.py:923
  97.9 10.0 %all_to_all.146.s_ref.sa_ref = f32[8,1,1024]{2,1,0:T(1,128)S(1)} all-to-all(f32[8,1,1024]{2,1,0:T(1,128)S(1)} %get-tuple-element.111), channel_id=1, replica_groups=mesh['batch'=8,'chan'=4] {'batch'}, dimensions={0} | all-to-all | bytes 65536 | tf_op jit(solution)/shard_map/all_to_all | solution.py:997
  118.3 9.0 %shard_map.309.k_ref = bf16[4,9,512,128]{3,2,1,0:T(8,128)(2,1)} custom-call(s32[1]{0:T(128)} %bitcast.12.c_ref, bf16[9,512,128]{2,1,0:T(8,128)(2,1)} %bitcast.17.refs_0_, bf16[9,512,128]{2,1,0:T(8,128)(2,1)} %collective-permute-done.8.refs_1_, bf16[9,512,128]{2,1,0:T(8,128)(2,1)} %collective-permute-done.9.refs_2_, ...), custom_call_target="tpu_custom_call" | custom-call | bytes 9437184 | tf_op jit(solution)/shard_map/pallas_call | solution.py:964
  132.1 9.4 %collective-permute-done.12.refs_2_ = bf16[512,512]{1,0:T(8,128)(2,1)} collective-permute-done((bf16[512,512]{1,0:T(8,128)(2,1)S(1)}, bf16[512,512]{1,0:T(8,128)(2,1)}, u32[]{:S(2)}, u32[]{:S(2)}) %collective-permute-start.12) | collective-permute-done | bytes 524320 | tf_op jit(solution)/shard_map/ppermute | solution.py:911
  141.5 6.8 shard_map.310
  149.2 12.4 %all_to_all.147.s_ref.sb_ref = f32[8,1,1024]{2,1,0:T(1,128)S(1)} all-to-all(f32[8,1,1024]{2,1,0:T(1,128)S(1)} %get-tuple-element.115), channel_id=1, replica_groups=mesh['batch'=8,'chan'=4] {'batch'}, dimensions={0} | all-to-all | bytes 65536 | tf_op jit(solution)/shard_map/all_to_all | solution.py:997
  169.3 12.3 %collective-permute-done.15.refs_2_ = bf16[2048,128]{1,0:T(8,128)(2,1)S(1)} collective-permute-done((bf16[2048,128]{1,0:T(8,128)(2,1)}, bf16[2048,128]{1,0:T(8,128)(2,1)S(1)}, u32[]{:S(2)}, u32[]{:S(2)}) %collective-permute-start.15) | collective-permute-done | bytes 524320 | tf_op jit(solution)/shard_map/ppermute | solution.py:911
  213.4 6.1 shard_map.315
  221.2 6.0 all-to-all-start.7
  227.2 9.0 %shard_map.316.k_ref = bf16[4,9,512,128]{3,2,1,0:T(8,128)(2,1)} custom-call(s32[1]{0:T(128)} %bitcast.12.c_ref, bf16[9,512,128]{2,1,0:T(8,128)(2,1)} %bitcast.24.refs_0_, bf16[9,512,128]{2,1,0:T(8,128)(2,1)} %collective-permute-done.17.refs_1_, bf16[9,512,128]{2,1,0:T(8,128)(2,1)} %bitcast.25.refs_2_, bf16[9,512,128]{2,1,0:T(8,128)(2,1)} %collective-permute-done.18.refs_3_), custom_call_target="tpu_custom_call" | custom-call | bytes 9437184 | tf_op jit(solution)/shard_map/pallas_call | solution.py:964
  244.7 6.0 all-to-all-start.9
  265.3 7.3 all-to-all-done.11.s_ref.sf_ref
  272.6 24.1 %all_to_all.148.ct_ref = bf16[4,392,512]{2,1,0:T(8,128)(2,1)S(1)} all-to-all(bf16[4,392,512]{2,1,0:T(8,128)(2,1)} %bitcast.151), channel_id=1, replica_groups=mesh['batch'=8,'chan'=4] {'chan'}, dimensions={0} | all-to-all | bytes 3211264 | tf_op jit(solution)/shard_map/all_to_all | solution.py:981
  296.8 5.9 shard_map.320
  307.8 7.3 all-to-all-done.14.gf_ref
  378.8 8.3 %shard_map.326 = (bf16[392,512]{1,0:T(8,128)(2,1)S(1)}, f32[392,2048]{1,0:T(8,128)}, f32[8,1,6144]{2,1,0:T(1,128)S(1)}) custom-call(f32[3]{0:T(128)S(1)} %copy-done.102, f32[392,512]{1,0:T(8,128)S(1)} %copy-done.60, f32[392,512]{1,0:T(8,128)S(1)} %copy-done.28, f32[8,1,1024]{2,1,0:T(1,128)S(1)} %copy-done.84, f32[8,1,1024]{2,1,0:T(1,128)} %all-to-all-done.16.gd_ref, ...), custom_call_target="tpu_custom_call" | custom-call | flops 822083584 | bytes 16547840 | tf_op jit(solution)/shard_map/pallas_call | solution.py:26
  418.1 6.8 shard_map.329
  426.5 6.2 all-to-all-start.18
  456.2 8.7 %shard_map.333 = (bf16[392,512]{1,0:T(8,128)(2,1)S(1)}, f32[4,392,512]{2,1,0:T(8,128)S(1)}, f32[8,1,1024]{2,1,0:T(1,128)}) custom-call(f32[3]{0:T(128)S(1)} %copy-done.104, f32[392,512]{1,0:T(8,128)S(1)} %copy-done.62, f32[392,512]{1,0:T(8,128)S(1)} %copy-done.32, f32[8,1,1024]{2,1,0:T(1,128)S(1)} %copy-done.81, f32[8,1,1024]{2,1,0:T(1,128)S(1)} %all-to-all-done.18.gb_ref, ...), custom_call_target="tpu_custom_call" | custom-call | flops 1849688064 | bytes 11141120 | tf_op jit(solution)/shard_map/pallas_call | solution.py:26
  467.4 6.0 all-to-all-start.19
  504.2 6.6 shard_map.338
  515.0 6.0 all-to-all-start.27
  521.3 14.6 %all-to-all-done.27 = bf16[8,64,512]{2,1,0:T(8,128)(2,1)} async-done(((bf16[8,64,512]{2,1,0:T(8,128)(2,1)}), bf16[8,64,512]{2,1,0:T(8,128)(2,1)}, u32[]{:S(2)}, u32[]{:S(2)}) %all-to-all-start.27) | async-done | bytes 524320 | tf_op jit(solution)/shard_map/all_to_all | solution.py:1108
  535.8 7.3 all_to_all.149
  554.8 7.2 collective-permute-done.30
  576.9 14.0 %all_to_all.150 = bf16[8,64,512]{2,1,0:T(8,128)(2,1)} all-to-all(bf16[8,64,512]{2,1,0:T(8,128)(2,1)S(1)} %bitcast.150), channel_id=1, replica_groups=mesh['batch'=8,'chan'=4] {'batch'}, dimensions={0} | all-to-all | bytes 1048576 | tf_op jit(solution)/shard_map/all_to_all | solution.py:1108
  595.3 24.3 %all-to-all-done.26 = bf16[8,9,64,128]{3,2,1,0:T(8,128)(2,1)} async-done(((bf16[8,9,64,128]{3,2,1,0:T(8,128)(2,1)}), bf16[8,9,64,128]{3,2,1,0:T(8,128)(2,1)}, u32[]{:S(2)}, u32[]{:S(2)}) %all-to-all-start.26) | async-done | bytes 1179680 | tf_op jit(solution)/shard_map/all_to_all | solution.py:1108
  631.4 53.4 %collective-permute-done.34 = bf16[1024,512]{1,0:T(8,128)(2,1)S(1)} collective-permute-done((bf16[1024,512]{1,0:T(8,128)(2,1)}, bf16[1024,512]{1,0:T(8,128)(2,1)S(1)}, u32[]{:S(2)}, u32[]{:S(2)}) %collective-permute-start.34) | collective-permute-done | bytes 1048608 | tf_op jit(solution)/shard_map/ppermute | solution.py:1095
  689.7 20.1 %collective-permute-done.32 = bf16[4608,128]{1,0:T(8,128)(2,1)} collective-permute-done((bf16[4608,128]{1,0:T(8,128)(2,1)S(1)}, bf16[4608,128]{1,0:T(8,128)(2,1)}, u32[]{:S(2)}, u32[]{:S(2)}) %collective-permute-start.32) | collective-permute-done | bytes 1179680 | tf_op jit(solution)/shard_map/ppermute | solution.py:1095
  732.1 15.4 %all-to-all-done.22 = bf16[8,9,64,128]{3,2,1,0:T(8,128)(2,1)S(1)} async-done(((bf16[8,9,64,128]{3,2,1,0:T(8,128)(2,1)}), bf16[8,9,64,128]{3,2,1,0:T(8,128)(2,1)S(1)}, u32[]{:S(2)}, u32[]{:S(2)}) %all-to-all-start.22) | async-done | bytes 1179680 | tf_op jit(solution)/shard_map/all_to_all | solution.py:1108
  (493 shorter events, 344.1 us)
Async XLA Ops:
  65.8 32.1 %all-to-all-start.2 = ((bf16[8,128,512]{2,1,0:T(8,128)(2,1)}), bf16[8,128,512]{2,1,0:T(8,128)(2,1)}, u32[]{:S(2)}, u32[]{:S(2)}) async-start(bf16[8,128,512]{2,1,0:T(8,128)(2,1)} %broadcast_in_dim.23), calls=%async_computation.2 | async-start | bytes 2097152 | tf_op jit(solution)/shard_map/all_to_all | solution.py:923
  72.0 41.4 %collective-permute-start.9 = (bf16[9,512,128]{2,1,0:T(8,128)(2,1)}, bf16[9,512,128]{2,1,0:T(8,128)(2,1)}, u32[]{:S(2)}, u32[]{:S(2)}) collective-permute-start(bf16[9,512,128]{2,1,0:T(8,128)(2,1)} %bitcast.17.refs_0_), channel_id=1, source_target_pairs={{0,2},{1,3},{2,0},{3,1},{4,6},{5,7},{6,4},{7,5},{8,10},{9,11},{10,... | collective-permute-start | bytes 3538952 | tf_op jit(solution)/shard_map/ppermute | solution.py:911
  109.1 40.2 %all-to-all-start.8 = ((bf16[8,576,128]{2,1,0:T(8,128)(2,1)}), bf16[8,576,128]{2,1,0:T(8,128)(2,1)}, u32[]{:S(2)}, u32[]{:S(2)}) async-start(bf16[8,576,128]{2,1,0:T(8,128)(2,1)} %broadcast_in_dim.25), calls=%async_computation.8 | async-start | bytes 2359296 | tf_op jit(solution)/shard_map/all_to_all | solution.py:923
  114.4 52.3 %collective-permute-start.11 = (bf16[512,512]{1,0:T(8,128)(2,1)}, bf16[512,512]{1,0:T(8,128)(2,1)}, u32[]{:S(2)}, u32[]{:S(2)}) collective-permute-start(bf16[512,512]{1,0:T(8,128)(2,1)} %refs_0_.7), channel_id=1, source_target_pairs={{0,1},{1,0},{2,3},{3,2},{4,5},{5,4},{6,7},{7,6},{8,9},{9,8},{10,11... | collective-permute-start | bytes 1572872 | tf_op jit(solution)/shard_map/ppermute | solution.py:930
  141.5 25.2 %collective-permute-start.13 = (bf16[512,512]{1,0:T(8,128)(2,1)}, bf16[512,512]{1,0:T(8,128)(2,1)}, u32[]{:S(2)}, u32[]{:S(2)}) collective-permute-start(bf16[512,512]{1,0:T(8,128)(2,1)} %collective-permute-done.12.refs_2_), channel_id=1, source_target_pairs={{0,1},{1,0},{2,3},{3,2},{4,5},{5,4},{6,7},{7,6},{8,9},{9,8},{10,11... | collective-permute-start | bytes 1572872 | tf_op jit(solution)/shard_map/ppermute | solution.py:930
  162.5 24.9 %all-to-all-start.10 = ((bf16[8,64,512]{2,1,0:T(8,128)(2,1)}), bf16[8,64,512]{2,1,0:T(8,128)(2,1)}, u32[]{:S(2)}, u32[]{:S(2)}) async-start(bf16[8,64,512]{2,1,0:T(8,128)(2,1)} %broadcast_in_dim.26), calls=%async_computation.10 | async-start | bytes 1048576 | tf_op jit(solution)/shard_map/all_to_all | solution.py:923
  168.8 58.4 %collective-permute-start.17 = (bf16[9,512,128]{2,1,0:T(8,128)(2,1)}, bf16[9,512,128]{2,1,0:T(8,128)(2,1)}, u32[]{:S(2)}, u32[]{:S(2)}) collective-permute-start(bf16[9,512,128]{2,1,0:T(8,128)(2,1)} %bitcast.24.refs_0_), channel_id=1, source_target_pairs={{0,1},{1,0},{2,3},{3,2},{4,5},{5,4},{6,7},{7,6},{8,9},{9,8},{10,11... | collective-permute-start | bytes 3538952 | tf_op jit(solution)/shard_map/ppermute | solution.py:930
  168.8 58.4 %collective-permute-start.18 = (bf16[9,512,128]{2,1,0:T(8,128)(2,1)}, bf16[9,512,128]{2,1,0:T(8,128)(2,1)}, u32[]{:S(2)}, u32[]{:S(2)}) collective-permute-start(bf16[9,512,128]{2,1,0:T(8,128)(2,1)} %bitcast.25.refs_2_), channel_id=1, source_target_pairs={{0,1},{1,0},{2,3},{3,2},{4,5},{5,4},{6,7},{7,6},{8,9},{9,8},{10,11... | collective-permute-start | bytes 3538952 | tf_op jit(solution)/shard_map/ppermute | solution.py:930
  169.3 36.8 %collective-permute-start.14 = (bf16[2048,128]{1,0:T(8,128)(2,1)}, bf16[2048,128]{1,0:T(8,128)(2,1)S(1)}, u32[]{:S(2)}, u32[]{:S(2)}) collective-permute-start(bf16[2048,128]{1,0:T(8,128)(2,1)} %refs_0_.8), channel_id=1, source_target_pairs={{0,1},{1,0},{2,3},{3,2},{4,5},{5,4},{6,7},{7,6},{8,9},{9,8},{10,11... | collective-permute-start | bytes 1572872 | tf_op jit(solution)/shard_map/ppermute | solution.py:930
  181.6 25.7 %collective-permute-start.16 = (bf16[2048,128]{1,0:T(8,128)(2,1)S(1)}, bf16[2048,128]{1,0:T(8,128)(2,1)S(1)}, u32[]{:S(2)}, u32[]{:S(2)}) collective-permute-start(bf16[2048,128]{1,0:T(8,128)(2,1)S(1)} %collective-permute-done.15.refs_2_), channel_id=1, source_target_pairs={{0,1},{1,0},{2,3},{3,2},{4,5},{5,4},{6,7},{7,6},{8,9},{9,8},{10,11... | collective-permute-start | bytes 1572872 | tf_op jit(solution)/shard_map/ppermute | solution.py:930
  206.0 44.7 %collective-permute-start.19 = (bf16[512,512]{1,0:T(8,128)(2,1)}, bf16[512,512]{1,0:T(8,128)(2,1)}, u32[]{:S(2)}, u32[]{:S(2)}) collective-permute-start(bf16[512,512]{1,0:T(8,128)(2,1)} %refs_0_.9), channel_id=1, source_target_pairs={{0,1},{1,0},{2,3},{3,2},{4,5},{5,4},{6,7},{7,6},{8,9},{9,8},{10,11... | collective-permute-start | bytes 1572872 | tf_op jit(solution)/shard_map/ppermute | solution.py:930
  206.9 43.9 %collective-permute-start.20 = (bf16[512,512]{1,0:T(8,128)(2,1)}, bf16[512,512]{1,0:T(8,128)(2,1)}, u32[]{:S(2)}, u32[]{:S(2)}) collective-permute-start(bf16[512,512]{1,0:T(8,128)(2,1)} %bitcast.28.refs_2_), channel_id=1, source_target_pairs={{0,1},{1,0},{2,3},{3,2},{4,5},{5,4},{6,7},{7,6},{8,9},{9,8},{10,11... | collective-permute-start | bytes 1572872 | tf_op jit(solution)/shard_map/ppermute | solution.py:930
  340.4 26.7 %collective-permute-start.21 = (bf16[2,512,512]{2,1,0:T(8,128)(2,1)}, bf16[2,512,512]{2,1,0:T(8,128)(2,1)}, u32[]{:S(2)}, u32[]{:S(2)}) collective-permute-start(bf16[2,512,512]{2,1,0:T(8,128)(2,1)} %copy-done.58), channel_id=1, source_target_pairs={{0,1},{1,0},{2,3},{3,2},{4,5},{5,4},{6,7},{7,6},{8,9},{9,8},{10,11... | collective-permute-start | bytes 3145736 | tf_op jit(solution)/shard_map/ppermute | solution.py:1083
  371.2 29.2 %collective-permute-start.23 = (bf16[2,4608,128]{2,1,0:T(8,128)(2,1)}, bf16[2,4608,128]{2,1,0:T(8,128)(2,1)}, u32[]{:S(2)}, u32[]{:S(2)}) collective-permute-start(bf16[2,4608,128]{2,1,0:T(8,128)(2,1)} %copy-done.40), channel_id=1, source_target_pairs={{0,1},{1,0},{2,3},{3,2},{4,5},{5,4},{6,7},{7,6},{8,9},{9,8},{10,11... | collective-permute-start | bytes 7077896 | tf_op jit(solution)/shard_map/ppermute | solution.py:1083
  371.7 26.6 %collective-permute-start.22 = (bf16[512,512]{1,0:T(8,128)(2,1)}, bf16[512,512]{1,0:T(8,128)(2,1)}, u32[]{:S(2)}, u32[]{:S(2)}) collective-permute-start(bf16[512,512]{1,0:T(8,128)(2,1)} %copy-done.127), channel_id=1, source_target_pairs={{0,2},{1,3},{2,0},{3,1},{4,6},{5,7},{6,4},{7,5},{8,10},{9,11},{10,... | collective-permute-start | bytes 1572872 | tf_op jit(solution)/shard_map/ppermute | solution.py:1095
  407.3 41.2 %collective-permute-start.24 = (bf16[2,2048,128]{2,1,0:T(8,128)(2,1)}, bf16[2,2048,128]{2,1,0:T(8,128)(2,1)}, u32[]{:S(2)}, u32[]{:S(2)}) collective-permute-start(bf16[2,2048,128]{2,1,0:T(8,128)(2,1)} %shard_map.328), channel_id=1, source_target_pairs={{0,1},{1,0},{2,3},{3,2},{4,5},{5,4},{6,7},{7,6},{8,9},{9,8},{10,11... | collective-permute-start | bytes 3145736 | tf_op jit(solution)/shard_map/ppermute | solution.py:1083
  410.2 75.1 %collective-permute-start.25 = (bf16[4608,128]{1,0:T(8,128)(2,1)}, bf16[4608,128]{1,0:T(8,128)(2,1)}, u32[]{:S(2)}, u32[]{:S(2)}) collective-permute-start(bf16[4608,128]{1,0:T(8,128)(2,1)} %get-tuple-element.175), channel_id=1, source_target_pairs={{0,2},{1,3},{2,0},{3,1},{4,6},{5,7},{6,4},{7,5},{8,10},{9,11},{10,... | collective-permute-start | bytes 3538952 | tf_op jit(solution)/shard_map/ppermute | solution.py:1095
  426.5 26.5 %all-to-all-start.18 = ((f32[8,1,1024]{2,1,0:T(1,128)}), f32[8,1,1024]{2,1,0:T(1,128)S(1)}, u32[]{:S(2)}, u32[]{:S(2)}) async-start(f32[8,1,1024]{2,1,0:T(1,128)} %copy-done.114), calls=%async_computation.18 | async-start | bytes 65536 | tf_op jit(solution)/shard_map/all_to_all | solution.py:997
  453.0 41.5 %collective-permute-start.28 = (bf16[2,1024,512]{2,1,0:T(8,128)(2,1)}, bf16[2,1024,512]{2,1,0:T(8,128)(2,1)}, u32[]{:S(2)}, u32[]{:S(2)}) collective-permute-start(bf16[2,1024,512]{2,1,0:T(8,128)(2,1)} %copy-done.41), channel_id=1, source_target_pairs={{0,1},{1,0},{2,3},{3,2},{4,5},{5,4},{6,7},{7,6},{8,9},{9,8},{10,11... | collective-permute-start | bytes 6291464 | tf_op jit(solution)/shard_map/ppermute | solution.py:1083
  453.0 37.4 %collective-permute-start.27 = (bf16[2,512,512]{2,1,0:T(8,128)(2,1)}, bf16[2,512,512]{2,1,0:T(8,128)(2,1)}, u32[]{:S(2)}, u32[]{:S(2)}) collective-permute-start(bf16[2,512,512]{2,1,0:T(8,128)(2,1)} %copy-done.57), channel_id=1, source_target_pairs={{0,1},{1,0},{2,3},{3,2},{4,5},{5,4},{6,7},{7,6},{8,9},{9,8},{10,11... | collective-permute-start | bytes 3145736 | tf_op jit(solution)/shard_map/ppermute | solution.py:1083
  453.5 34.9 %collective-permute-start.26 = (bf16[2048,128]{1,0:T(8,128)(2,1)}, bf16[2048,128]{1,0:T(8,128)(2,1)}, u32[]{:S(2)}, u32[]{:S(2)}) collective-permute-start(bf16[2048,128]{1,0:T(8,128)(2,1)} %copy-done.126), channel_id=1, source_target_pairs={{0,2},{1,3},{2,0},{3,1},{4,6},{5,7},{6,4},{7,5},{8,10},{9,11},{10,... | collective-permute-start | bytes 1572872 | tf_op jit(solution)/shard_map/ppermute | solution.py:1095
  480.9 34.1 %all-to-all-start.13 = ((bf16[4,392,512]{2,1,0:T(8,128)(2,1)}), bf16[4,392,512]{2,1,0:T(8,128)(2,1)}, u32[]{:S(2)}, u32[]{:S(2)}) async-start(bf16[4,392,512]{2,1,0:T(8,128)(2,1)} %copy-done.48), calls=%async_computation.13 | async-start | bytes 3211264 | tf_op jit(solution)/shard_map/all_to_all | solution.py:985
  514.6 32.7 %collective-permute-start.29 = (bf16[2,1024,128]{2,1,0:T(8,128)(2,1)}, bf16[2,1024,128]{2,1,0:T(8,128)(2,1)}, u32[]{:S(2)}, u32[]{:S(2)}) collective-permute-start(bf16[2,1024,128]{2,1,0:T(8,128)(2,1)} %shard_map.339), channel_id=1, source_target_pairs={{0,1},{1,0},{2,3},{3,2},{4,5},{5,4},{6,7},{7,6},{8,9},{9,8},{10,11... | collective-permute-start | bytes 1572872 | tf_op jit(solution)/shard_map/ppermute | solution.py:1083
  515.0 20.8 %all-to-all-start.27 = ((bf16[8,64,512]{2,1,0:T(8,128)(2,1)}), bf16[8,64,512]{2,1,0:T(8,128)(2,1)}, u32[]{:S(2)}, u32[]{:S(2)}) async-start(bf16[8,64,512]{2,1,0:T(8,128)(2,1)} %bitcast.148), calls=%async_computation.27 | async-start | bytes 1048576 | tf_op jit(solution)/shard_map/all_to_all | solution.py:1108
  543.1 19.7 %all-to-all-start.25 = ((bf16[8,256,128]{2,1,0:T(8,128)(2,1)}), bf16[8,256,128]{2,1,0:T(8,128)(2,1)}, u32[]{:S(2)}, u32[]{:S(2)}) async-start(bf16[8,256,128]{2,1,0:T(8,128)(2,1)} %bitcast.149), calls=%async_computation.25 | async-start | bytes 1048576 | tf_op jit(solution)/shard_map/all_to_all | solution.py:1108
  590.9 28.7 %all-to-all-start.26 = ((bf16[8,9,64,128]{3,2,1,0:T(8,128)(2,1)}), bf16[8,9,64,128]{3,2,1,0:T(8,128)(2,1)}, u32[]{:S(2)}, u32[]{:S(2)}) async-start(bf16[8,9,64,128]{3,2,1,0:T(8,128)(2,1)} %bitcast.145), calls=%async_computation.26 | async-start | bytes 2359296 | tf_op jit(solution)/shard_map/all_to_all | solution.py:1108
  595.2 31.2 %collective-permute-start.31 = (bf16[2,4608,128]{2,1,0:T(8,128)(2,1)S(1)}, bf16[2,4608,128]{2,1,0:T(8,128)(2,1)}, u32[]{:S(2)}, u32[]{:S(2)}) collective-permute-start(bf16[2,4608,128]{2,1,0:T(8,128)(2,1)S(1)} %copy-done.39), channel_id=1, source_target_pairs={{0,1},{1,0},{2,3},{3,2},{4,5},{5,4},{6,7},{7,6},{8,9},{9,8},{10,11... | collective-permute-start | bytes 7077896 | tf_op jit(solution)/shard_map/ppermute | solution.py:1083
  619.6 66.6 %all-to-all-start.20 = ((bf16[4,4,392,256]{3,2,1,0:T(8,128)(2,1)}), bf16[4,4,392,256]{3,2,1,0:T(8,128)(2,1)}, u32[]{:S(2)}, u32[]{:S(2)}) async-start(bf16[4,4,392,256]{3,2,1,0:T(8,128)(2,1)} %get-tuple-element.188), calls=%async_computation.20 | async-start | bytes 6422528 | tf_op jit(solution)/shard_map/all_to_all | solution.py:985
  624.4 60.5 %collective-permute-start.34 = (bf16[1024,512]{1,0:T(8,128)(2,1)}, bf16[1024,512]{1,0:T(8,128)(2,1)S(1)}, u32[]{:S(2)}, u32[]{:S(2)}) collective-permute-start(bf16[1024,512]{1,0:T(8,128)(2,1)} %copy-done.125), channel_id=1, source_target_pairs={{0,2},{1,3},{2,0},{3,1},{4,6},{5,7},{6,4},{7,5},{8,10},{9,11},{10,... | collective-permute-start | bytes 3145736 | tf_op jit(solution)/shard_map/ppermute | solution.py:1095
  631.2 78.6 %collective-permute-start.32 = (bf16[4608,128]{1,0:T(8,128)(2,1)S(1)}, bf16[4608,128]{1,0:T(8,128)(2,1)}, u32[]{:S(2)}, u32[]{:S(2)}) collective-permute-start(bf16[4608,128]{1,0:T(8,128)(2,1)S(1)} %get-tuple-element.194), channel_id=1, source_target_pairs={{0,2},{1,3},{2,0},{3,1},{4,6},{5,7},{6,4},{7,5},{8,10},{9,11},{10,... | collective-permute-start | bytes 3538952 | tf_op jit(solution)/shard_map/ppermute | solution.py:1095
  686.1 29.0 %all-to-all-start.24 = ((bf16[8,128,512]{2,1,0:T(8,128)(2,1)}), bf16[8,128,512]{2,1,0:T(8,128)(2,1)S(1)}, u32[]{:S(2)}, u32[]{:S(2)}) async-start(bf16[8,128,512]{2,1,0:T(8,128)(2,1)} %bitcast.65), calls=%async_computation.24 | async-start | bytes 2097152 | tf_op jit(solution)/shard_map/all_to_all | solution.py:1108
  715.2 32.3 %all-to-all-start.22 = ((bf16[8,9,64,128]{3,2,1,0:T(8,128)(2,1)}), bf16[8,9,64,128]{3,2,1,0:T(8,128)(2,1)S(1)}, u32[]{:S(2)}, u32[]{:S(2)}) async-start(bf16[8,9,64,128]{3,2,1,0:T(8,128)(2,1)} %bitcast.107), calls=%async_computation.22 | async-start | bytes 2359296 | tf_op jit(solution)/shard_map/all_to_all | solution.py:1108
  (173 other events, 1498.7 us)
